TPU v7x, 32 devices: a whole 2x2x4 slice. The times are simulated.
32 devices in a mesh: groups: 2 (over y), leaf: 16 (over z, x, core).
Axes of the slice: x: 2, y: 2, z: 4, core: 2. Of those that a mesh axis runs over, the one named last changes fastest.
Arguments:
- rhs: bfloat16 [64, 32768], P('groups', 'leaf'), parts along dimension 0, may hold values from -6 to 6
- bases: bfloat16 [512, 32, 128], P(('groups', 'leaf')), parts along dimension 0, may hold values from -0.5 to 0.5
- transfers: bfloat16 [512, 32, 32], P(('groups', 'leaf')), parts along dimension 0, may hold values from -0.5 to 0.5
- near_slots: int32 [32, 8, 8, 2], P(('groups', 'leaf')), parts along dimension 0, may hold values from -1 to 15, as said below
- near_blocks: bfloat16 [32, 8, 8, 128, 128], P(('groups', 'leaf')), parts along dimension 0, may hold values from -0.078125 to 0.078125
- local_pairs: int32 [32, 288, 2], P(('groups', 'leaf')), parts along dimension 0, may hold values from 0 to 15
- local_blocks: bfloat16 [32, 288, 128, 128], P(('groups', 'leaf')), parts along dimension 0, may hold values from -0.078125 to 0.078125
- far_slots: int32 [32, 8, 2, 2], P(('groups', 'leaf')), parts along dimension 0, may hold values from -1 to 15, as said below
- far_blocks: bfloat16 [32, 8, 2, 32, 32], P(('groups', 'leaf')), parts along dimension 0, may hold values from -0.75 to 0.75
- parent_pairs: int32 [32, 4], P(('groups', 'leaf')), parts along dimension 0, may hold values from -1 to 15, as said below
- parent_blocks: bfloat16 [32, 4, 32, 32], P(('groups', 'leaf')), parts along dimension 0, may hold values from -0.25 to 0.25
Outputs:
- first: bfloat16 [64, 32768], P('groups', 'leaf'), parts along dimension 0
- second: bfloat16 [64, 32768], P('groups', 'leaf'), parts along dimension 0
There are 2 independent parts, one for each index of `groups`. A program takes and returns all parts, laid end to end along the dimension named above; each array names one. Nothing has to cross between parts.
Inputs may be any that keep to these rules, and one draw needn't show every extreme that they name: near_slots[d, k, c] concerns neighbour k of owner d: entry 0 is owner d's local target leaf and entry 1 the neighbour's local source leaf, both -1 for an empty slot and for every neighbour outside 0 to 15; on every owner one existing neighbour fills all 8 slots. far_slots[d, k, c] concerns neighbour k of owner d in the same way, both entries -1 for an empty slot and for every neighbour outside 0 to 15; on every owner one existing neighbour fills all 2 slots. `parent_pairs`: the partner owner of each stored parent coupling block, -1 for an empty slot.
All inputs are finite; a program needn't handle non-finite values.
Results may differ from a plain program's by a relative error of at most 0.0065.
Values may be sent and summed in bfloat16 or wider, within the bound.
A program may use at most 128 MiB of HBM per device.

v0:
```python
import jax
import jax.numpy as jnp
from jax import lax
from jax.sharding import PartitionSpec as P


def shifted(shard, axis, by):
    size = lax.axis_size(axis)
    pairs = [(i, i + by) for i in range(size) if 0 <= i + by < size]
    return lax.ppermute(shard, axis, pairs)


def neighbour_offsets(count):
    half = count // 2
    return [step - half if step < half else step - half + 1 for step in range(count)]


def pick_rows(source_table, slot_index):
    safe_index = jnp.maximum(slot_index, 0).reshape(-1)
    picked = jnp.take(source_table, safe_index, axis=0)
    return picked.reshape(slot_index.shape + source_table.shape[1:])


def spread_rows(values, slot_index, row_count):
    flat_index = slot_index.reshape(-1)
    onehot = (flat_index[:, None] == jnp.arange(row_count, dtype=jnp.int32)[None, :]).astype(
        jnp.float32
    )
    flat_values = values.reshape((flat_index.shape[0],) + values.shape[slot_index.ndim :])
    return jnp.einsum("jl,j...->l...", onehot, flat_values, precision=lax.Precision.HIGHEST)


def apply_operator(
    field_now,
    near_req,
    far_req,
    bases,
    transfers,
    near_slots,
    near_blocks,
    local_pairs,
    local_blocks,
    far_slots,
    far_blocks,
    parent_pairs,
    parent_blocks,
):
    leaves = bases.shape[0]
    rank_width = bases.shape[1]
    rhs_count = field_now.shape[1]
    panel_width = field_now.shape[2]
    neigh_count = near_slots.shape[1]
    near_cap = near_slots.shape[2]
    far_cap = far_slots.shape[2]
    field_size = rhs_count * panel_width
    offsets = neighbour_offsets(neigh_count)
    peer_count = lax.axis_size("leaf")
    coef = jnp.einsum("lap,lrp->lar", bases, field_now, preferred_element_type=jnp.float32).astype(
        jnp.bfloat16
    )
    near_target = near_slots[0, :, :, 0]
    near_source = near_slots[0, :, :, 1]
    far_target = far_slots[0, :, :, 0]
    far_source = far_slots[0, :, :, 1]
    field_flat = field_now.reshape(leaves, field_size)
    coef_flat = coef.reshape(leaves, rank_width * rhs_count)
    packed = jnp.concatenate([field_flat, coef_flat], axis=1)
    received = []
    for step in range(neigh_count):
        received.append(shifted(packed, "leaf", -offsets[step]))
    peer_all = jnp.stack(received)
    fetched = jax.vmap(pick_rows)(peer_all[:, :, :field_size], near_source).reshape(
        neigh_count, near_cap, rhs_count, panel_width
    )
    far_fetched = jax.vmap(pick_rows)(peer_all[:, :, field_size:], far_source).reshape(
        neigh_count, far_cap, rank_width, rhs_count
    )
    near_tiles = near_blocks[0]
    live_mask = (near_target >= 0).astype(jnp.float32)[:, :, None, None]
    into_target = (
        jnp.einsum("pcrq,pcqk->pcrk", fetched, near_tiles, preferred_element_type=jnp.float32)
        * live_mask
    )
    target_rows = pick_rows(field_now, near_target)
    into_source = (
        jnp.einsum("pcrk,pcqk->pcrq", target_rows, near_tiles, preferred_element_type=jnp.float32)
        * live_mask
    ).astype(jnp.bfloat16)
    far_tiles = far_blocks[0]
    far_mask = (far_target >= 0).astype(jnp.float32)[:, :, None, None]
    far_into_target = (
        jnp.einsum("pcab,pcbr->pcar", far_tiles, far_fetched, preferred_element_type=jnp.float32)
        * far_mask
    )
    target_coef = pick_rows(coef, far_target)
    far_into_source = (
        jnp.einsum("pcab,pcar->pcbr", far_tiles, target_coef, preferred_element_type=jnp.float32)
        * far_mask
    ).astype(jnp.bfloat16)
    near_list = []
    far_list = []
    for step in range(neigh_count):
        near_list.append(shifted(into_source[neigh_count - 1 - step], "leaf", -offsets[step]))
    for step in range(neigh_count):
        far_list.append(shifted(far_into_source[neigh_count - 1 - step], "leaf", -offsets[step]))
    near_got = jnp.stack(near_list)
    far_got = jnp.stack(far_list)
    local_index = local_pairs[0]
    local_tiles = local_blocks[0]
    local_source = pick_rows(field_now, local_index[:, 1])
    local_target = pick_rows(field_now, local_index[:, 0])
    local_into_target = jnp.einsum(
        "krq,kqm->krm", local_source, local_tiles, preferred_element_type=jnp.float32
    )
    local_into_source = jnp.einsum(
        "krm,kqm->krq", local_target, local_tiles, preferred_element_type=jnp.float32
    )
    near_sum = spread_rows(into_target, near_target, leaves) + spread_rows(
        near_got.astype(jnp.float32), near_req, leaves
    )
    near_sum = near_sum + spread_rows(local_into_target, local_index[:, 0], leaves)
    near_sum = near_sum + spread_rows(local_into_source, local_index[:, 1], leaves)
    far_sum = spread_rows(far_into_target, far_target, leaves) + spread_rows(
        far_got.astype(jnp.float32), far_req, leaves
    )
    parent = jnp.einsum("lab,lbr->ar", transfers, coef, preferred_element_type=jnp.float32).astype(
        jnp.bfloat16
    )
    all_parents = lax.all_gather(parent[None], "leaf", axis=0, tiled=True)
    partner_ids = parent_pairs[0]
    parent_mask = (partner_ids >= 0).astype(jnp.float32)[:, None, None]
    parent_mats = parent_blocks[0]
    partner_coef = pick_rows(all_parents, partner_ids)
    own_part = jnp.sum(
        jnp.einsum("jab,jbr->jar", parent_mats, partner_coef, preferred_element_type=jnp.float32)
        * parent_mask,
        axis=0,
    )
    returned = (
        jnp.einsum("jab,ar->jbr", parent_mats, parent, preferred_element_type=jnp.float32)
        * parent_mask
    )
    return_rows = spread_rows(returned, partner_ids, peer_count)
    parent_total = (
        own_part + lax.psum_scatter(return_rows, "leaf", scatter_dimension=0, tiled=True)[0]
    )
    parent_half = parent_total.astype(jnp.bfloat16)
    lifted = jnp.einsum("lab,ar->lbr", transfers, parent_half, preferred_element_type=jnp.float32)
    down_half = (far_sum + lifted).astype(jnp.bfloat16)
    result = near_sum + jnp.einsum(
        "lar,lap->lrp", down_half, bases, preferred_element_type=jnp.float32
    )
    return result.astype(jnp.bfloat16)


def body(
    rhs,
    bases,
    transfers,
    near_slots,
    near_blocks,
    local_pairs,
    local_blocks,
    far_slots,
    far_blocks,
    parent_pairs,
    parent_blocks,
):
    leaves = bases.shape[0]
    panel_width = bases.shape[2]
    rhs_count = rhs.shape[0]
    neigh_count = near_slots.shape[1]
    near_cap = near_slots.shape[2]
    offsets = neighbour_offsets(neigh_count)
    wanted = jnp.concatenate([near_slots[0, :, :, 1], far_slots[0, :, :, 1]], axis=1)
    asked = []
    for step in range(neigh_count):
        asked.append(shifted(wanted[neigh_count - 1 - step], "leaf", -offsets[step]))
    asked_all = jnp.stack(asked)
    near_req = asked_all[:, :near_cap]
    far_req = asked_all[:, near_cap:]
    field_now = rhs.reshape(rhs_count, leaves, panel_width).transpose(1, 0, 2)
    extra = (
        bases,
        transfers,
        near_slots,
        near_blocks,
        local_pairs,
        local_blocks,
        far_slots,
        far_blocks,
        parent_pairs,
        parent_blocks,
    )
    first_leaf = apply_operator(field_now, near_req, far_req, *extra)
    second_leaf = apply_operator(first_leaf, near_req, far_req, *extra)
    first = first_leaf.transpose(1, 0, 2).reshape(rhs_count, leaves * panel_width)
    second = second_leaf.transpose(1, 0, 2).reshape(rhs_count, leaves * panel_width)
    return (first, second)


def solution(mesh):
    in_specs = (
        P("groups", "leaf"),
        P(("groups", "leaf"), None, None),
        P(("groups", "leaf"), None, None),
        P(("groups", "leaf"), None, None, None),
        P(("groups", "leaf"), None, None, None, None),
        P(("groups", "leaf"), None, None),
        P(("groups", "leaf"), None, None, None),
        P(("groups", "leaf"), None, None, None),
        P(("groups", "leaf"), None, None, None, None),
        P(("groups", "leaf"), None),
        P(("groups", "leaf"), None, None, None),
    )
    out_specs = (P("groups", "leaf"), P("groups", "leaf"))
    return jax.shard_map(body, mesh=mesh, in_specs=in_specs, out_specs=out_specs, check_vma=False)
```

profile of v0, /device:TPU:0, one launch (start us, length us, event | category | flops | bytes accessed | tf_op | source)
XLA Modules:
  0.0 465.3 jit_solution(18061157288868048653)
XLA Ops:
  11.0 5.6 %collective-permute-start = (bf16[16,5120]{1,0:T(8,128)(2,1)}, bf16[16,5120]{1,0:T(8,128)(2,1)}, u32[]{:S(2)}, u32[]{:S(2)}) collective-permute-start(bf16[16,5120]{1,0:T(8,128)(2,1)} %constant_dynamic-update-slice_fusion), channel_id=1, source_target_pairs={{0,4},{1,5},{2,6},{3,7},{4,8},{5,9},{6,10},{7,11},{8,12},{9,13},{1... | collective-permute-start | bytes 491528 | tf_op jit(solution)/shard_map/ppermute | solution.py:10
  16.6 3.2 collective-permute-start.1
  38.7 18.3 %all-gather = bf16[512,32]{1,0:T(8,128)(2,1)S(1)} all-gather(bf16[32,32]{1,0:T(8,128)(2,1)S(1)} %copy.126), channel_id=2, replica_groups=mesh['groups'=2,'leaf'=16] {'leaf'}, dimensions={0}, use_global_device_ids=true | all-gather | bytes 34816 | tf_op jit(solution)/shard_map/all_gather | solution.py:129
  60.0 7.9 %fusion.4 = f32[288,32,128]{2,1,0:T(8,128)S(1)} fusion(bf16[1,288,128,128]{3,2,1,0:T(8,128)(2,1)} %param.29, bf16[288,32,128]{2,1,0:T(8,128)(2,1)} %gather_fusion.3, pred[288]{0:T(512)(128)(4,1)S(1)} %broadcast_compare_fusion), kind=kOutput, calls=%fused_computation.18 | convolution fusion | flops 303169536 | bytes 16515360 | tf_op jit(solution)/shard_map/krm,kqm->krq/dot_general | solution.py:115
  68.0 5.1 %fusion.12 = f32[16,32,128]{2,0,1:T(8,128)} fusion(f32[288,32,128]{2,1,0:T(8,128)S(1)} %fusion.4, s32[288]{0:T(512)S(1)} %get-tuple-element.4), kind=kOutput, calls=%fused_computation.26 | convolution fusion | flops 226497024 | bytes 4981888 | tf_op jit(solution)/shard_map/jl,j...->l.../dot_general | solution.py:30
  76.7 9.2 %fusion.6 = f32[288,32,128]{2,1,0:T(8,128)} fusion(bf16[1,288,128,128]{3,2,1,0:T(8,128)(2,1)} %param.29, bf16[288,32,128]{2,1,0:T(8,128)(2,1)} %gather_fusion.2, pred[288]{0:T(512)(128)(4,1)S(1)} %broadcast_compare_fusion.1), kind=kOutput, calls=%fused_computation.20 | convolution fusion | flops 303169536 | bytes 16515360 | tf_op jit(solution)/shard_map/krq,kqm->krm/dot_general | solution.py:112
  87.2 3.3 collective-permute-start.9
  94.4 3.7 collective-permute-start.11
  103.1 5.0 %collective-permute-done.13 = s32[10]{0:T(128)S(1)} collective-permute-done((s32[10]{0:T(128)S(1)}, s32[10]{0:T(128)S(1)}, u32[]{:S(2)}, u32[]{:S(2)}) %collective-permute-start.13) | collective-permute-done | bytes 72 | tf_op jit(solution)/shard_map/ppermute | solution.py:10
  109.4 6.9 %collective-permute-done.14 = s32[10]{0:T(128)S(1)} collective-permute-done((s32[10]{0:T(128)S(1)}, s32[10]{0:T(128)S(1)}, u32[]{:S(2)}, u32[]{:S(2)}) %collective-permute-start.14) | collective-permute-done | bytes 72 | tf_op jit(solution)/shard_map/ppermute | solution.py:10
  117.6 4.1 collective-permute-done.15
  125.0 4.6 collective-permute-start.25
  131.2 3.9 collective-permute-start.26
  140.0 4.3 collective-permute-done.28
  145.7 5.3 %collective-permute-done.29 = bf16[2,32,32]{1,2,0:T(8,128)(2,1)S(1)} collective-permute-done((bf16[2,32,32]{1,2,0:T(8,128)(2,1)S(1)}, bf16[2,32,32]{1,2,0:T(8,128)(2,1)S(1)}, u32[]{:S(2)}, u32[]{:S(2)}) %collective-permute-start.29) | collective-permute-done | bytes 4128 | tf_op jit(solution)/shard_map/ppermute | solution.py:10
  152.2 5.6 %collective-permute-done.30 = bf16[2,32,32]{1,2,0:T(8,128)(2,1)S(1)} collective-permute-done((bf16[2,32,32]{1,2,0:T(8,128)(2,1)S(1)}, bf16[2,32,32]{1,2,0:T(8,128)(2,1)S(1)}, u32[]{:S(2)}, u32[]{:S(2)}) %collective-permute-start.30) | collective-permute-done | bytes 4128 | tf_op jit(solution)/shard_map/ppermute | solution.py:10
  159.1 4.3 collective-permute-done.31
  163.4 3.6 collective-permute-start.16
  177.3 3.6 collective-permute-start.19
  183.7 4.4 collective-permute-done.20
  190.5 5.1 %collective-permute-done.21 = bf16[8,32,128]{2,1,0:T(8,128)(2,1)S(1)} collective-permute-done((bf16[8,32,128]{2,1,0:T(8,128)(2,1)S(1)}, bf16[8,32,128]{2,1,0:T(8,128)(2,1)S(1)}, u32[]{:S(2)}, u32[]{:S(2)}) %collective-permute-start.21) | collective-permute-done | bytes 65568 | tf_op jit(solution)/shard_map/ppermute | solution.py:10
  197.6 7.6 %collective-permute-done.22 = bf16[8,32,128]{2,1,0:T(8,128)(2,1)S(1)} collective-permute-done((bf16[8,32,128]{2,1,0:T(8,128)(2,1)S(1)}, bf16[8,32,128]{2,1,0:T(8,128)(2,1)S(1)}, u32[]{:S(2)}, u32[]{:S(2)}) %collective-permute-start.22) | collective-permute-done | bytes 65568 | tf_op jit(solution)/shard_map/ppermute | solution.py:10
  207.1 4.2 collective-permute-done.23
  220.5 3.8 collective-permute-done.5
  225.9 6.4 %collective-permute-done.7 = bf16[16,5120]{1,0:T(8,128)(2,1)S(1)} collective-permute-done((bf16[16,5120]{1,0:T(8,128)(2,1)}, bf16[16,5120]{1,0:T(8,128)(2,1)S(1)}, u32[]{:S(2)}, u32[]{:S(2)}) %collective-permute-start.7) | collective-permute-done | bytes 163872 | tf_op jit(solution)/shard_map/ppermute | solution.py:10
  233.1 3.0 gather_fusion
  245.4 6.6 %fusion.74 = bf16[16,32,128]{2,0,1:T(8,128)(2,1)S(1)} fusion(f32[16,32,128]{2,0,1:T(8,128)S(1)} %copy-done.7, f32[16,32,128]{2,0,1:T(8,128)S(1)} %convolution_add_fusion.1, f32[288,32,128]{2,1,0:T(8,128)} %fusion.6, f32[16,32,128]{2,1,0:T(8,128)S(1)} %fusion.113, s32[288]{0:T(512)} %copy-done.21), kind=kOutput, calls=%fused_computation.74 | convolution fusion | flops 226759168 | bytes 5637248 | tf_op jit(solution)/shard_map/jl,j...->l.../dot_general | solution.py:30
  255.1 3.9 collective-permute-start.32
  261.9 4.1 collective-permute-start.34
  279.5 17.5 %all-gather.1 = bf16[512,32]{1,0:T(8,128)(2,1)S(1)} all-gather(bf16[32,32]{1,0:T(8,128)(2,1)S(1)} %copy.150), channel_id=3, replica_groups=mesh['groups'=2,'leaf'=16] {'leaf'}, dimensions={0}, use_global_device_ids=true | all-gather | bytes 34816 | tf_op jit(solution)/shard_map/all_gather | solution.py:129
  300.4 10.3 %fusion = f32[288,32,128]{2,1,0:T(8,128)} fusion(bf16[1,288,128,128]{3,2,1,0:T(8,128)(2,1)} %param.29, bf16[288,32,128]{2,1,0:T(8,128)(2,1)S(1)} %copy-done.2, pred[288]{0:T(512)(128)(4,1)} %copy-done.47), kind=kOutput, calls=%fused_computation.14 | convolution fusion | flops 303169536 | bytes 16515360 | tf_op jit(solution)/shard_map/krm,kqm->krq/dot_general | solution.py:115
  310.7 7.3 %fusion.8 = f32[16,32,128]{2,0,1:T(8,128)} fusion(f32[288,32,128]{2,1,0:T(8,128)} %fusion, s32[288]{0:T(512)} %copy-done.23), kind=kOutput, calls=%fused_computation.22 | convolution fusion | flops 226497024 | bytes 4981888 | tf_op jit(solution)/shard_map/jl,j...->l.../dot_general | solution.py:30
  318.2 4.3 fusion.2
  324.1 3.8 collective-permute-start.49
  332.1 4.1 collective-permute-start.51
  341.4 5.0 %collective-permute-done.53 = bf16[2,32,32]{1,2,0:T(8,128)(2,1)S(1)} collective-permute-done((bf16[2,32,32]{1,2,0:T(8,128)(2,1)S(1)}, bf16[2,32,32]{1,2,0:T(8,128)(2,1)S(1)}, u32[]{:S(2)}, u32[]{:S(2)}) %collective-permute-start.53) | collective-permute-done | bytes 4128 | tf_op jit(solution)/shard_map/ppermute | solution.py:10
  347.7 6.7 %collective-permute-done.54 = bf16[2,32,32]{1,2,0:T(8,128)(2,1)S(1)} collective-permute-done((bf16[2,32,32]{1,2,0:T(8,128)(2,1)S(1)}, bf16[2,32,32]{1,2,0:T(8,128)(2,1)S(1)}, u32[]{:S(2)}, u32[]{:S(2)}) %collective-permute-start.54) | collective-permute-done | bytes 4128 | tf_op jit(solution)/shard_map/ppermute | solution.py:10
  355.7 4.3 collective-permute-done.55
  360.0 3.1 collective-permute-start.40
  368.8 3.6 collective-permute-start.42
  374.2 3.6 collective-permute-start.43
  380.6 3.5 collective-permute-done.44
  386.1 5.6 %collective-permute-done.45 = bf16[8,32,128]{2,1,0:T(8,128)(2,1)S(1)} collective-permute-done((bf16[8,32,128]{2,1,0:T(8,128)(2,1)S(1)}, bf16[8,32,128]{2,1,0:T(8,128)(2,1)S(1)}, u32[]{:S(2)}, u32[]{:S(2)}) %collective-permute-start.45) | collective-permute-done | bytes 65568 | tf_op jit(solution)/shard_map/ppermute | solution.py:10
  393.6 7.6 %collective-permute-done.46 = bf16[8,32,128]{2,1,0:T(8,128)(2,1)S(1)} collective-permute-done((bf16[8,32,128]{2,1,0:T(8,128)(2,1)S(1)}, bf16[8,32,128]{2,1,0:T(8,128)(2,1)S(1)}, u32[]{:S(2)}, u32[]{:S(2)}) %collective-permute-start.46) | collective-permute-done | bytes 65568 | tf_op jit(solution)/shard_map/ppermute | solution.py:10
  403.3 4.2 collective-permute-done.47
  422.1 6.4 %collective-permute-done.39 = bf16[16,5120]{1,0:T(8,128)(2,1)S(1)} collective-permute-done((bf16[16,5120]{1,0:T(8,128)(2,1)}, bf16[16,5120]{1,0:T(8,128)(2,1)S(1)}, u32[]{:S(2)}, u32[]{:S(2)}) %collective-permute-start.39) | collective-permute-done | bytes 163872 | tf_op jit(solution)/shard_map/ppermute | solution.py:10
  443.8 3.0 gather_fusion.7
  451.0 6.5 %fusion.77 = bf16[16,32,128]{2,0,1:T(8,128)(2,1)S(1)} fusion(f32[16,32,128]{2,0,1:T(8,128)S(1)} %copy-done.8, f32[16,32,128]{2,0,1:T(8,128)S(1)} %convolution_add_fusion, f32[288,32,128]{2,1,0:T(8,128)} %fusion.2, f32[16,32,128]{2,1,0:T(8,128)S(1)} %copy-done.9, s32[288]{0:T(512)S(1)} %copy-done.22), kind=kOutput, calls=%fused_computation.75 | convolution fusion | flops 226759168 | bytes 5637248 | tf_op jit(solution)/shard_map/jl,j...->l.../dot_general | solution.py:30
  (391 shorter events, 182.2 us)
Async XLA Ops:
  7.2 206.0 %reduce-scatter.3.cloned.1.call-start = ((), (), s32[]{:S(2)}) async-start(), calls=%async_computation.2 | async-start | bytes 278528 | tf_op jit(solution)/shard_map/reduce_scatter | solution.py:145
  11.0 203.6 %collective-permute-start = (bf16[16,5120]{1,0:T(8,128)(2,1)}, bf16[16,5120]{1,0:T(8,128)(2,1)}, u32[]{:S(2)}, u32[]{:S(2)}) collective-permute-start(bf16[16,5120]{1,0:T(8,128)(2,1)} %constant_dynamic-update-slice_fusion), channel_id=1, source_target_pairs={{0,4},{1,5},{2,6},{3,7},{4,8},{5,9},{6,10},{7,11},{8,12},{9,13},{1... | collective-permute-start | bytes 491528 | tf_op jit(solution)/shard_map/ppermute | solution.py:10
  16.6 200.3 %collective-permute-start.1 = (bf16[16,5120]{1,0:T(8,128)(2,1)}, bf16[16,5120]{1,0:T(8,128)(2,1)}, u32[]{:S(2)}, u32[]{:S(2)}) collective-permute-start(bf16[16,5120]{1,0:T(8,128)(2,1)} %constant_dynamic-update-slice_fusion), channel_id=1, source_target_pairs={{0,3},{1,4},{2,5},{3,6},{4,7},{5,8},{6,9},{7,10},{8,11},{9,12},{10... | collective-permute-start | bytes 491528 | tf_op jit(solution)/shard_map/ppermute | solution.py:10
  19.8 199.3 %collective-permute-start.2 = (bf16[16,5120]{1,0:T(8,128)(2,1)}, bf16[16,5120]{1,0:T(8,128)(2,1)S(1)}, u32[]{:S(2)}, u32[]{:S(2)}) collective-permute-start(bf16[16,5120]{1,0:T(8,128)(2,1)} %constant_dynamic-update-slice_fusion), channel_id=1, source_target_pairs={{0,2},{1,3},{2,4},{3,5},{4,6},{5,7},{6,8},{7,9},{8,10},{9,11},{10,... | collective-permute-start | bytes 491528 | tf_op jit(solution)/shard_map/ppermute | solution.py:10
  24.3 62.8 %collective-permute-start.8 = (s32[10]{0:T(128)S(1)}, s32[10]{0:T(128)S(1)}, u32[]{:S(2)}, u32[]{:S(2)}) collective-permute-start(s32[10]{0:T(128)S(1)} %get-tuple-element.53), channel_id=1, source_target_pairs={{0,4},{1,5},{2,6},{3,7},{4,8},{5,9},{6,10},{7,11},{8,12},{9,13},{1... | collective-permute-start | bytes 128 | tf_op jit(solution)/shard_map/ppermute | solution.py:10
  30.7 93.7 %collective-permute-start.24 = (bf16[2,32,32]{1,2,0:T(8,128)(2,1)S(1)}, bf16[2,32,32]{1,2,0:T(8,128)(2,1)S(1)}, u32[]{:S(2)}, u32[]{:S(2)}) collective-permute-start(bf16[2,32,32]{1,2,0:T(8,128)(2,1)S(1)} %get-tuple-element.41), channel_id=1, source_target_pairs={{0,4},{1,5},{2,6},{3,7},{4,8},{5,9},{6,10},{7,11},{8,12},{9,13},{1... | collective-permute-start | bytes 12296 | tf_op jit(solution)/shard_map/ppermute | solution.py:10
  35.2 374.3 %reduce-scatter.5.cloned.1.call-start = ((), (), s32[]{:S(2)}) async-start(), calls=%async_computation.3 | async-start | bytes 278528 | tf_op jit(solution)/shard_map/reduce_scatter | solution.py:145
  87.2 4.6 collective-permute-start.9
  101.9 6.2 %collective-permute-start.13 = (s32[10]{0:T(128)S(1)}, s32[10]{0:T(128)S(1)}, u32[]{:S(2)}, u32[]{:S(2)}) collective-permute-start(s32[10]{0:T(128)S(1)} %get-tuple-element.48), channel_id=1, source_target_pairs={{2,0},{3,1},{4,2},{5,3},{6,4},{7,5},{8,6},{9,7},{10,8},{11,9},{12,... | collective-permute-start | bytes 128 | tf_op jit(solution)/shard_map/ppermute | solution.py:10
  108.1 8.2 %collective-permute-start.14 = (s32[10]{0:T(128)S(1)}, s32[10]{0:T(128)S(1)}, u32[]{:S(2)}, u32[]{:S(2)}) collective-permute-start(s32[10]{0:T(128)S(1)} %get-tuple-element.47), channel_id=1, source_target_pairs={{3,0},{4,1},{5,2},{6,3},{7,4},{8,5},{9,6},{10,7},{11,8},{12,9},{13... | collective-permute-start | bytes 128 | tf_op jit(solution)/shard_map/ppermute | solution.py:10
  116.3 5.4 %collective-permute-start.15 = (s32[10]{0:T(128)S(1)}, s32[10]{0:T(128)S(1)}, u32[]{:S(2)}, u32[]{:S(2)}) collective-permute-start(s32[10]{0:T(128)S(1)} %get-tuple-element.46), channel_id=1, source_target_pairs={{4,0},{5,1},{6,2},{7,3},{8,4},{9,5},{10,6},{11,7},{12,8},{13,9},{1... | collective-permute-start | bytes 128 | tf_op jit(solution)/shard_map/ppermute | solution.py:10
  121.8 98.7 %collective-permute-start.3 = (bf16[16,5120]{1,0:T(8,128)(2,1)}, bf16[16,5120]{1,0:T(8,128)(2,1)S(1)}, u32[]{:S(2)}, u32[]{:S(2)}) collective-permute-start(bf16[16,5120]{1,0:T(8,128)(2,1)} %constant_dynamic-update-slice_fusion), channel_id=1, source_target_pairs={{0,1},{1,2},{2,3},{3,4},{4,5},{5,6},{6,7},{7,8},{8,9},{9,10},{10,1... | collective-permute-start | bytes 491528 | tf_op jit(solution)/shard_map/ppermute | solution.py:10
  125.0 6.2 %collective-permute-start.25 = (bf16[2,32,32]{1,2,0:T(8,128)(2,1)}, bf16[2,32,32]{1,2,0:T(8,128)(2,1)S(1)}, u32[]{:S(2)}, u32[]{:S(2)}) collective-permute-start(bf16[2,32,32]{1,2,0:T(8,128)(2,1)} %get-tuple-element.40), channel_id=1, source_target_pairs={{0,3},{1,4},{2,5},{3,6},{4,7},{5,8},{6,9},{7,10},{8,11},{9,12},{10... | collective-permute-start | bytes 12296 | tf_op jit(solution)/shard_map/ppermute | solution.py:10
  131.2 5.4 %collective-permute-start.26 = (bf16[2,32,32]{1,2,0:T(8,128)(2,1)S(1)}, bf16[2,32,32]{1,2,0:T(8,128)(2,1)S(1)}, u32[]{:S(2)}, u32[]{:S(2)}) collective-permute-start(bf16[2,32,32]{1,2,0:T(8,128)(2,1)S(1)} %copy-done.33), channel_id=1, source_target_pairs={{0,2},{1,3},{2,4},{3,5},{4,6},{5,7},{6,8},{7,9},{8,10},{9,11},{10,... | collective-permute-start | bytes 12296 | tf_op jit(solution)/shard_map/ppermute | solution.py:10
  138.7 5.6 %collective-permute-start.28 = (bf16[2,32,32]{1,2,0:T(8,128)(2,1)S(1)}, bf16[2,32,32]{1,2,0:T(8,128)(2,1)S(1)}, u32[]{:S(2)}, u32[]{:S(2)}) collective-permute-start(bf16[2,32,32]{1,2,0:T(8,128)(2,1)S(1)} %copy-done.31), channel_id=1, source_target_pairs={{1,0},{2,1},{3,2},{4,3},{5,4},{6,5},{7,6},{8,7},{9,8},{10,9},{11,1... | collective-permute-start | bytes 12296 | tf_op jit(solution)/shard_map/ppermute | solution.py:10
  144.3 6.6 %collective-permute-start.29 = (bf16[2,32,32]{1,2,0:T(8,128)(2,1)S(1)}, bf16[2,32,32]{1,2,0:T(8,128)(2,1)S(1)}, u32[]{:S(2)}, u32[]{:S(2)}) collective-permute-start(bf16[2,32,32]{1,2,0:T(8,128)(2,1)S(1)} %get-tuple-element.36), channel_id=1, source_target_pairs={{2,0},{3,1},{4,2},{5,3},{6,4},{7,5},{8,6},{9,7},{10,8},{11,9},{12,... | collective-permute-start | bytes 12296 | tf_op jit(solution)/shard_map/ppermute | solution.py:10
  150.9 6.9 %collective-permute-start.30 = (bf16[2,32,32]{1,2,0:T(8,128)(2,1)S(1)}, bf16[2,32,32]{1,2,0:T(8,128)(2,1)S(1)}, u32[]{:S(2)}, u32[]{:S(2)}) collective-permute-start(bf16[2,32,32]{1,2,0:T(8,128)(2,1)S(1)} %get-tuple-element.35), channel_id=1, source_target_pairs={{3,0},{4,1},{5,2},{6,3},{7,4},{8,5},{9,6},{10,7},{11,8},{12,9},{13... | collective-permute-start | bytes 12296 | tf_op jit(solution)/shard_map/ppermute | solution.py:10
  157.8 5.6 %collective-permute-start.31 = (bf16[2,32,32]{1,2,0:T(8,128)(2,1)S(1)}, bf16[2,32,32]{1,2,0:T(8,128)(2,1)S(1)}, u32[]{:S(2)}, u32[]{:S(2)}) collective-permute-start(bf16[2,32,32]{1,2,0:T(8,128)(2,1)S(1)} %get-tuple-element.34), channel_id=1, source_target_pairs={{4,0},{5,1},{6,2},{7,3},{8,4},{9,5},{10,6},{11,7},{12,8},{13,9},{1... | collective-permute-start | bytes 12296 | tf_op jit(solution)/shard_map/ppermute | solution.py:10
  163.4 5.5 %collective-permute-start.16 = (bf16[8,32,128]{2,1,0:T(8,128)(2,1)S(1)}, bf16[8,32,128]{2,1,0:T(8,128)(2,1)S(1)}, u32[]{:S(2)}, u32[]{:S(2)}) collective-permute-start(bf16[8,32,128]{2,1,0:T(8,128)(2,1)S(1)} %get-tuple-element.25), channel_id=1, source_target_pairs={{0,4},{1,5},{2,6},{3,7},{4,8},{5,9},{6,10},{7,11},{8,12},{9,13},{1... | collective-permute-start | bytes 196616 | tf_op jit(solution)/shard_map/ppermute | solution.py:10
  172.5 4.9 %collective-permute-start.18 = (bf16[8,32,128]{2,1,0:T(8,128)(2,1)S(1)}, bf16[8,32,128]{2,1,0:T(8,128)(2,1)S(1)}, u32[]{:S(2)}, u32[]{:S(2)}) collective-permute-start(bf16[8,32,128]{2,1,0:T(8,128)(2,1)S(1)} %get-tuple-element.23), channel_id=1, source_target_pairs={{0,2},{1,3},{2,4},{3,5},{4,6},{5,7},{6,8},{7,9},{8,10},{9,11},{10,... | collective-permute-start | bytes 196616 | tf_op jit(solution)/shard_map/ppermute | solution.py:10
  181.8 6.3 %collective-permute-start.20 = (bf16[8,32,128]{2,1,0:T(8,128)(2,1)S(1)}, bf16[8,32,128]{2,1,0:T(8,128)(2,1)S(1)}, u32[]{:S(2)}, u32[]{:S(2)}) collective-permute-start(bf16[8,32,128]{2,1,0:T(8,128)(2,1)S(1)} %get-tuple-element.21), channel_id=1, source_target_pairs={{1,0},{2,1},{3,2},{4,3},{5,4},{6,5},{7,6},{8,7},{9,8},{10,9},{11,1... | collective-permute-start | bytes 196616 | tf_op jit(solution)/shard_map/ppermute | solution.py:10
  188.1 7.5 %collective-permute-start.21 = (bf16[8,32,128]{2,1,0:T(8,128)(2,1)S(1)}, bf16[8,32,128]{2,1,0:T(8,128)(2,1)S(1)}, u32[]{:S(2)}, u32[]{:S(2)}) collective-permute-start(bf16[8,32,128]{2,1,0:T(8,128)(2,1)S(1)} %get-tuple-element.20), channel_id=1, source_target_pairs={{2,0},{3,1},{4,2},{5,3},{6,4},{7,5},{8,6},{9,7},{10,8},{11,9},{12,... | collective-permute-start | bytes 196616 | tf_op jit(solution)/shard_map/ppermute | solution.py:10
  195.6 9.5 %collective-permute-start.22 = (bf16[8,32,128]{2,1,0:T(8,128)(2,1)S(1)}, bf16[8,32,128]{2,1,0:T(8,128)(2,1)S(1)}, u32[]{:S(2)}, u32[]{:S(2)}) collective-permute-start(bf16[8,32,128]{2,1,0:T(8,128)(2,1)S(1)} %get-tuple-element.19), channel_id=1, source_target_pairs={{3,0},{4,1},{5,2},{6,3},{7,4},{8,5},{9,6},{10,7},{11,8},{12,9},{13... | collective-permute-start | bytes 196616 | tf_op jit(solution)/shard_map/ppermute | solution.py:10
  205.2 6.1 %collective-permute-start.23 = (bf16[8,32,128]{2,1,0:T(8,128)(2,1)S(1)}, bf16[8,32,128]{2,1,0:T(8,128)(2,1)S(1)}, u32[]{:S(2)}, u32[]{:S(2)}) collective-permute-start(bf16[8,32,128]{2,1,0:T(8,128)(2,1)S(1)} %get-tuple-element.18), channel_id=1, source_target_pairs={{4,0},{5,1},{6,2},{7,3},{8,4},{9,5},{10,6},{11,7},{12,8},{13,9},{1... | collective-permute-start | bytes 196616 | tf_op jit(solution)/shard_map/ppermute | solution.py:10
  211.3 9.2 %collective-permute-start.4 = (bf16[16,5120]{1,0:T(8,128)(2,1)}, bf16[16,5120]{1,0:T(8,128)(2,1)S(1)}, u32[]{:S(2)}, u32[]{:S(2)}) collective-permute-start(bf16[16,5120]{1,0:T(8,128)(2,1)} %constant_dynamic-update-slice_fusion), channel_id=1, source_target_pairs={{1,0},{2,1},{3,2},{4,3},{5,4},{6,5},{7,6},{8,7},{9,8},{10,9},{11,1... | collective-permute-start | bytes 491528 | tf_op jit(solution)/shard_map/ppermute | solution.py:10
  214.6 9.7 %collective-permute-start.5 = (bf16[16,5120]{1,0:T(8,128)(2,1)}, bf16[16,5120]{1,0:T(8,128)(2,1)S(1)}, u32[]{:S(2)}, u32[]{:S(2)}) collective-permute-start(bf16[16,5120]{1,0:T(8,128)(2,1)} %constant_dynamic-update-slice_fusion), channel_id=1, source_target_pairs={{2,0},{3,1},{4,2},{5,3},{6,4},{7,5},{8,6},{9,7},{10,8},{11,9},{12,... | collective-permute-start | bytes 491528 | tf_op jit(solution)/shard_map/ppermute | solution.py:10
  216.9 9.0 %collective-permute-start.6 = (bf16[16,5120]{1,0:T(8,128)(2,1)}, bf16[16,5120]{1,0:T(8,128)(2,1)S(1)}, u32[]{:S(2)}, u32[]{:S(2)}) collective-permute-start(bf16[16,5120]{1,0:T(8,128)(2,1)} %constant_dynamic-update-slice_fusion), channel_id=1, source_target_pairs={{3,0},{4,1},{5,2},{6,3},{7,4},{8,5},{9,6},{10,7},{11,8},{12,9},{13... | collective-permute-start | bytes 491528 | tf_op jit(solution)/shard_map/ppermute | solution.py:10
  219.1 13.2 %collective-permute-start.7 = (bf16[16,5120]{1,0:T(8,128)(2,1)}, bf16[16,5120]{1,0:T(8,128)(2,1)S(1)}, u32[]{:S(2)}, u32[]{:S(2)}) collective-permute-start(bf16[16,5120]{1,0:T(8,128)(2,1)} %constant_dynamic-update-slice_fusion), channel_id=1, source_target_pairs={{4,0},{5,1},{6,2},{7,3},{8,4},{9,5},{10,6},{11,7},{12,8},{13,9},{1... | collective-permute-start | bytes 491528 | tf_op jit(solution)/shard_map/ppermute | solution.py:10
  255.1 155.8 %collective-permute-start.32 = (bf16[16,5120]{1,0:T(8,128)(2,1)}, bf16[16,5120]{1,0:T(8,128)(2,1)}, u32[]{:S(2)}, u32[]{:S(2)}) collective-permute-start(bf16[16,5120]{1,0:T(8,128)(2,1)} %constant_dynamic-update-slice_fusion.17), channel_id=1, source_target_pairs={{0,4},{1,5},{2,6},{3,7},{4,8},{5,9},{6,10},{7,11},{8,12},{9,13},{1... | collective-permute-start | bytes 491528 | tf_op jit(solution)/shard_map/ppermute | solution.py:10
  259.0 154.1 %collective-permute-start.33 = (bf16[16,5120]{1,0:T(8,128)(2,1)}, bf16[16,5120]{1,0:T(8,128)(2,1)}, u32[]{:S(2)}, u32[]{:S(2)}) collective-permute-start(bf16[16,5120]{1,0:T(8,128)(2,1)} %constant_dynamic-update-slice_fusion.17), channel_id=1, source_target_pairs={{0,3},{1,4},{2,5},{3,6},{4,7},{5,8},{6,9},{7,10},{8,11},{9,12},{10... | collective-permute-start | bytes 491528 | tf_op jit(solution)/shard_map/ppermute | solution.py:10
  261.9 153.4 %collective-permute-start.34 = (bf16[16,5120]{1,0:T(8,128)(2,1)}, bf16[16,5120]{1,0:T(8,128)(2,1)}, u32[]{:S(2)}, u32[]{:S(2)}) collective-permute-start(bf16[16,5120]{1,0:T(8,128)(2,1)} %constant_dynamic-update-slice_fusion.17), channel_id=1, source_target_pairs={{0,2},{1,3},{2,4},{3,5},{4,6},{5,7},{6,8},{7,9},{8,10},{9,11},{10,... | collective-permute-start | bytes 491528 | tf_op jit(solution)/shard_map/ppermute | solution.py:10
  266.0 151.6 %collective-permute-start.35 = (bf16[16,5120]{1,0:T(8,128)(2,1)}, bf16[16,5120]{1,0:T(8,128)(2,1)}, u32[]{:S(2)}, u32[]{:S(2)}) collective-permute-start(bf16[16,5120]{1,0:T(8,128)(2,1)} %constant_dynamic-update-slice_fusion.17), channel_id=1, source_target_pairs={{0,1},{1,2},{2,3},{3,4},{4,5},{5,6},{6,7},{7,8},{8,9},{9,10},{10,1... | collective-permute-start | bytes 491528 | tf_op jit(solution)/shard_map/ppermute | solution.py:10
  276.0 48.0 %collective-permute-start.48 = (bf16[2,32,32]{1,2,0:T(8,128)(2,1)}, bf16[2,32,32]{1,2,0:T(8,128)(2,1)}, u32[]{:S(2)}, u32[]{:S(2)}) collective-permute-start(bf16[2,32,32]{1,2,0:T(8,128)(2,1)} %get-tuple-element.33), channel_id=1, source_target_pairs={{0,4},{1,5},{2,6},{3,7},{4,8},{5,9},{6,10},{7,11},{8,12},{9,13},{1... | collective-permute-start | bytes 12296 | tf_op jit(solution)/shard_map/ppermute | solution.py:10
  324.1 5.3 %collective-permute-start.49 = (bf16[2,32,32]{1,2,0:T(8,128)(2,1)S(1)}, bf16[2,32,32]{1,2,0:T(8,128)(2,1)S(1)}, u32[]{:S(2)}, u32[]{:S(2)}) collective-permute-start(bf16[2,32,32]{1,2,0:T(8,128)(2,1)S(1)} %copy-done.40), channel_id=1, source_target_pairs={{0,3},{1,4},{2,5},{3,6},{4,7},{5,8},{6,9},{7,10},{8,11},{9,12},{10... | collective-permute-start | bytes 12296 | tf_op jit(solution)/shard_map/ppermute | solution.py:10
  332.1 4.9 %collective-permute-start.51 = (bf16[2,32,32]{1,2,0:T(8,128)(2,1)S(1)}, bf16[2,32,32]{1,2,0:T(8,128)(2,1)S(1)}, u32[]{:S(2)}, u32[]{:S(2)}) collective-permute-start(bf16[2,32,32]{1,2,0:T(8,128)(2,1)S(1)} %copy-done.38), channel_id=1, source_target_pairs={{0,1},{1,2},{2,3},{3,4},{4,5},{5,6},{6,7},{7,8},{8,9},{9,10},{10,1... | collective-permute-start | bytes 12296 | tf_op jit(solution)/shard_map/ppermute | solution.py:10
  340.1 6.3 %collective-permute-start.53 = (bf16[2,32,32]{1,2,0:T(8,128)(2,1)S(1)}, bf16[2,32,32]{1,2,0:T(8,128)(2,1)S(1)}, u32[]{:S(2)}, u32[]{:S(2)}) collective-permute-start(bf16[2,32,32]{1,2,0:T(8,128)(2,1)S(1)} %copy-done.36), channel_id=1, source_target_pairs={{2,0},{3,1},{4,2},{5,3},{6,4},{7,5},{8,6},{9,7},{10,8},{11,9},{12,... | collective-permute-start | bytes 12296 | tf_op jit(solution)/shard_map/ppermute | solution.py:10
  346.4 8.0 %collective-permute-start.54 = (bf16[2,32,32]{1,2,0:T(8,128)(2,1)S(1)}, bf16[2,32,32]{1,2,0:T(8,128)(2,1)S(1)}, u32[]{:S(2)}, u32[]{:S(2)}) collective-permute-start(bf16[2,32,32]{1,2,0:T(8,128)(2,1)S(1)} %copy-done.35), channel_id=1, source_target_pairs={{3,0},{4,1},{5,2},{6,3},{7,4},{8,5},{9,6},{10,7},{11,8},{12,9},{13... | collective-permute-start | bytes 12296 | tf_op jit(solution)/shard_map/ppermute | solution.py:10
  354.4 5.6 %collective-permute-start.55 = (bf16[2,32,32]{1,2,0:T(8,128)(2,1)S(1)}, bf16[2,32,32]{1,2,0:T(8,128)(2,1)S(1)}, u32[]{:S(2)}, u32[]{:S(2)}) collective-permute-start(bf16[2,32,32]{1,2,0:T(8,128)(2,1)S(1)} %copy-done.34), channel_id=1, source_target_pairs={{4,0},{5,1},{6,2},{7,3},{8,4},{9,5},{10,6},{11,7},{12,8},{13,9},{1... | collective-permute-start | bytes 12296 | tf_op jit(solution)/shard_map/ppermute | solution.py:10
  360.0 5.0 %collective-permute-start.40 = (bf16[8,32,128]{2,1,0:T(8,128)(2,1)S(1)}, bf16[8,32,128]{2,1,0:T(8,128)(2,1)S(1)}, u32[]{:S(2)}, u32[]{:S(2)}) collective-permute-start(bf16[8,32,128]{2,1,0:T(8,128)(2,1)S(1)} %copy-done.20), channel_id=1, source_target_pairs={{0,4},{1,5},{2,6},{3,7},{4,8},{5,9},{6,10},{7,11},{8,12},{9,13},{1... | collective-permute-start | bytes 196616 | tf_op jit(solution)/shard_map/ppermute | solution.py:10
  368.8 5.5 %collective-permute-start.42 = (bf16[8,32,128]{2,1,0:T(8,128)(2,1)S(1)}, bf16[8,32,128]{2,1,0:T(8,128)(2,1)S(1)}, u32[]{:S(2)}, u32[]{:S(2)}) collective-permute-start(bf16[8,32,128]{2,1,0:T(8,128)(2,1)S(1)} %copy-done.18), channel_id=1, source_target_pairs={{0,2},{1,3},{2,4},{3,5},{4,6},{5,7},{6,8},{7,9},{8,10},{9,11},{10,... | collective-permute-start | bytes 196616 | tf_op jit(solution)/shard_map/ppermute | solution.py:10
  378.7 5.5 %collective-permute-start.44 = (bf16[8,32,128]{2,1,0:T(8,128)(2,1)S(1)}, bf16[8,32,128]{2,1,0:T(8,128)(2,1)S(1)}, u32[]{:S(2)}, u32[]{:S(2)}) collective-permute-start(bf16[8,32,128]{2,1,0:T(8,128)(2,1)S(1)} %copy-done.16), channel_id=1, source_target_pairs={{1,0},{2,1},{3,2},{4,3},{5,4},{6,5},{7,6},{8,7},{9,8},{10,9},{11,1... | collective-permute-start | bytes 196616 | tf_op jit(solution)/shard_map/ppermute | solution.py:10
  384.2 7.5 %collective-permute-start.45 = (bf16[8,32,128]{2,1,0:T(8,128)(2,1)S(1)}, bf16[8,32,128]{2,1,0:T(8,128)(2,1)S(1)}, u32[]{:S(2)}, u32[]{:S(2)}) collective-permute-start(bf16[8,32,128]{2,1,0:T(8,128)(2,1)S(1)} %get-tuple-element.12), channel_id=1, source_target_pairs={{2,0},{3,1},{4,2},{5,3},{6,4},{7,5},{8,6},{9,7},{10,8},{11,9},{12,... | collective-permute-start | bytes 196616 | tf_op jit(solution)/shard_map/ppermute | solution.py:10
  391.7 9.5 %collective-permute-start.46 = (bf16[8,32,128]{2,1,0:T(8,128)(2,1)S(1)}, bf16[8,32,128]{2,1,0:T(8,128)(2,1)S(1)}, u32[]{:S(2)}, u32[]{:S(2)}) collective-permute-start(bf16[8,32,128]{2,1,0:T(8,128)(2,1)S(1)} %get-tuple-element.10), channel_id=1, source_target_pairs={{3,0},{4,1},{5,2},{6,3},{7,4},{8,5},{9,6},{10,7},{11,8},{12,9},{13... | collective-permute-start | bytes 196616 | tf_op jit(solution)/shard_map/ppermute | solution.py:10
  401.2 6.3 %collective-permute-start.47 = (bf16[8,32,128]{2,1,0:T(8,128)(2,1)S(1)}, bf16[8,32,128]{2,1,0:T(8,128)(2,1)S(1)}, u32[]{:S(2)}, u32[]{:S(2)}) collective-permute-start(bf16[8,32,128]{2,1,0:T(8,128)(2,1)S(1)} %get-tuple-element.8), channel_id=1, source_target_pairs={{4,0},{5,1},{6,2},{7,3},{8,4},{9,5},{10,6},{11,7},{12,8},{13,9},{1... | collective-permute-start | bytes 196616 | tf_op jit(solution)/shard_map/ppermute | solution.py:10
  407.6 11.0 %collective-permute-start.36 = (bf16[16,5120]{1,0:T(8,128)(2,1)}, bf16[16,5120]{1,0:T(8,128)(2,1)S(1)}, u32[]{:S(2)}, u32[]{:S(2)}) collective-permute-start(bf16[16,5120]{1,0:T(8,128)(2,1)} %constant_dynamic-update-slice_fusion.17), channel_id=1, source_target_pairs={{1,0},{2,1},{3,2},{4,3},{5,4},{6,5},{7,6},{8,7},{9,8},{10,9},{11,1... | collective-permute-start | bytes 491528 | tf_op jit(solution)/shard_map/ppermute | solution.py:10
  410.9 9.6 %collective-permute-start.37 = (bf16[16,5120]{1,0:T(8,128)(2,1)}, bf16[16,5120]{1,0:T(8,128)(2,1)S(1)}, u32[]{:S(2)}, u32[]{:S(2)}) collective-permute-start(bf16[16,5120]{1,0:T(8,128)(2,1)} %constant_dynamic-update-slice_fusion.17), channel_id=1, source_target_pairs={{2,0},{3,1},{4,2},{5,3},{6,4},{7,5},{8,6},{9,7},{10,8},{11,9},{12,... | collective-permute-start | bytes 491528 | tf_op jit(solution)/shard_map/ppermute | solution.py:10
  413.1 9.0 %collective-permute-start.38 = (bf16[16,5120]{1,0:T(8,128)(2,1)}, bf16[16,5120]{1,0:T(8,128)(2,1)S(1)}, u32[]{:S(2)}, u32[]{:S(2)}) collective-permute-start(bf16[16,5120]{1,0:T(8,128)(2,1)} %constant_dynamic-update-slice_fusion.17), channel_id=1, source_target_pairs={{3,0},{4,1},{5,2},{6,3},{7,4},{8,5},{9,6},{10,7},{11,8},{12,9},{13... | collective-permute-start | bytes 491528 | tf_op jit(solution)/shard_map/ppermute | solution.py:10
  415.4 13.2 %collective-permute-start.39 = (bf16[16,5120]{1,0:T(8,128)(2,1)}, bf16[16,5120]{1,0:T(8,128)(2,1)S(1)}, u32[]{:S(2)}, u32[]{:S(2)}) collective-permute-start(bf16[16,5120]{1,0:T(8,128)(2,1)} %constant_dynamic-update-slice_fusion.17), channel_id=1, source_target_pairs={{4,0},{5,1},{6,2},{7,3},{8,4},{9,5},{10,6},{11,7},{12,8},{13,9},{1... | collective-permute-start | bytes 491528 | tf_op jit(solution)/shard_map/ppermute | solution.py:10
  (79 other events, 1223.8 us)
Sparse Core Ops, SparseCore 0:
  35.4 52.6 reduce-scatter.2
  279.5 52.5 reduce-scatter.4
where the time goes:
time: 471 us; the launch traced here: 465 us
  waiting for transfers between devices  136 us (29%)
  starting transfers between devices  121 us (26%)
  matrix products  81.2 us (17%)
  local copies, waits for them, and re-layouts  68.7 us (15%)
  blocking collectives  35.8 us (8%)
  between operations  15.9 us (3%)
  other arithmetic  6.22 us (1%)
    ppermute x56, waiting for transfers between devices, shifted(): return lax.ppermute(shard, axis, pairs)  136 us
    ppermute x56, starting transfers between devices, shifted(): return lax.ppermute(shard, axis, pairs)  121 us
    all_gather x2, blocking collectives, apply_operator(): all_parents = lax.all_gather(parent[None], 'leaf', axis=0, tiled=True)  35.8 us
    dot_general x14, matrix products, spread_rows(): jnp.einsum('jl,j...->l...', onehot, flat_values, precision=lax.Precision....  35.8 us
    gather x19, local copies, waits for them, and re-layouts, pick_rows(): picked = jnp.take(source_table, safe_index, axis=0)  27.5 us
    unnamed x185, local copies, waits for them, and re-layouts  19.9 us
    dot_general x2, matrix products, apply_operator(): jnp.einsum('krm,kqm->krq', local_target, local_tiles, preferred_element_t...  18.2 us
    dot_general x2, matrix products, apply_operator(): jnp.einsum('krq,kqm->krm', local_source, local_tiles, preferred_element_t...  13.5 us
  transfers between devices with their start and end apart: 58, of which 43 were waited for; matrix products, arithmetic and copies ran while one was open for 21% of the time, Pallas kernels for 0%

commit v1 on v0

v1 whole, which is shorter than its diff:
```python
import jax
import jax.numpy as jnp
from jax import lax
from jax.experimental import pallas as pl
from jax.experimental.pallas import tpu as pltpu
from jax.sharding import PartitionSpec as P

F32 = jnp.float32
BF16 = jnp.bfloat16
NN = (((1,), (0,)), ((), ()))
NT = (((1,), (1,)), ((), ()))
TN = (((0,), (0,)), ((), ()))


def mm(a, b, dims=NN):
    return lax.dot_general(a, b, dims, preferred_element_type=F32)


def shifted(shard, axis, by):
    size = lax.axis_size(axis)
    pairs = [(i, i + by) for i in range(size) if 0 <= i + by < size]
    return lax.ppermute(shard, axis, pairs)


def neighbour_offsets(count):
    half = count // 2
    return [step - half if step < half else step - half + 1 for step in range(count)]


def vmem():
    return pl.BlockSpec(memory_space=pltpu.VMEM)


def smem():
    return pl.BlockSpec(memory_space=pltpu.SMEM)


def leaf_cols(ref, leaf, width):
    return ref[:, pl.ds(pl.multiple_of(leaf * width, width), width)]


def params():
    return pltpu.CompilerParams(vmem_limit_bytes=40 * 1024 * 1024)


def start_kernel(x_ref, bases_ref, transfers_ref, v_ref, u_ref):
    leaves, _, width = bases_ref.shape
    for leaf in range(leaves):
        v_ref[:, leaf * width : (leaf + 1) * width] = mm(
            transfers_ref[leaf], bases_ref[leaf]
        ).astype(BF16)
    u_ref[...] = mm(x_ref[...], v_ref[...], NT).astype(BF16)


def start_call(x, bases, transfers):
    rank = bases.shape[1]
    return pl.pallas_call(
        start_kernel,
        out_shape=(
            jax.ShapeDtypeStruct((rank, x.shape[1]), BF16),
            jax.ShapeDtypeStruct((x.shape[0], rank), BF16),
        ),
        in_specs=[vmem()] * 3,
        out_specs=(vmem(), vmem()),
        compiler_params=params(),
        cost_estimate=pl.CostEstimate(flops=10**7, bytes_accessed=10**6, transcendentals=0),
        name="parent_basis",
    )(x, bases, transfers)


def local_kernel(unroll, pairs_ref, x_ref, blocks_ref, out_ref, *accs):
    step = pl.program_id(0)
    per_step, width = blocks_ref.shape[0], blocks_ref.shape[1]

    @pl.when(step == 0)
    def _():
        for acc in accs:
            acc[...] = jnp.zeros_like(acc)

    def group(i, carry):
        base = i * unroll
        work = []
        for j in range(unroll):
            place = (step * per_step + base + j) * 2
            target, source = pairs_ref[place], pairs_ref[place + 1]
            block = blocks_ref[base + j]
            work.append(
                (
                    target,
                    source,
                    mm(leaf_cols(x_ref, source, width), block),
                    mm(leaf_cols(x_ref, target, width), block, NT),
                )
            )
        for j, (target, source, to_target, to_source) in enumerate(work):
            first, second = accs[2 * (j % 2)], accs[2 * (j % 2) + 1]
            first[target] += to_target
            second[source] += to_source
        return carry

    lax.fori_loop(0, per_step // unroll, group, 0)

    @pl.when(step == pl.num_programs(0) - 1)
    def _():
        out_ref[...] = (accs[0][...] + accs[1][...]) + (accs[2][...] + accs[3][...])


def local_call(x, pairs, blocks):
    count, width = blocks.shape[0], blocks.shape[1]
    leaves = x.shape[1] // width
    steps = next(s for s in (6, 4, 3, 2, 1) if count % s == 0)
    per_step = count // steps
    unroll = next(s for s in (8, 6, 4, 3, 2, 1) if per_step % s == 0)
    shape = (leaves, x.shape[0], width)

    def kernel(*refs):
        local_kernel(unroll, *refs)

    return pl.pallas_call(
        kernel,
        grid=(steps,),
        out_shape=jax.ShapeDtypeStruct(shape, F32),
        in_specs=[
            smem(),
            vmem(),
            pl.BlockSpec((per_step, width, width), lambda i: (i, 0, 0)),
        ],
        out_specs=vmem(),
        scratch_shapes=[pltpu.VMEM(shape, F32)] * 4,
        compiler_params=params(),
        cost_estimate=pl.CostEstimate(
            flops=count * 4 * 32 * width * width * 16,
            bytes_accessed=blocks.size * 2,
            transcendentals=0,
        ),
        name="local_blocks",
    )(pairs.reshape(-1), x, blocks)


def far_kernel(neigh, cap, slots_ref, back_ref, mine_ref, far_ref, *refs):
    peers, got = refs[:neigh], refs[neigh : 2 * neigh]
    ahead_ref, behind_ref = refs[2 * neigh :]
    for k in range(neigh):
        for c in range(cap):
            place = (k * cap + c) * 2
            target = jnp.maximum(slots_ref[place], 0)
            source = jnp.maximum(slots_ref[place + 1], 0)
            lifted = mm(far_ref[k, c], mine_ref[target], TN).astype(BF16)
            ahead_ref[k, c] = mm(peers[k][source], lifted, TN).astype(BF16)
            target = jnp.maximum(back_ref[place], 0)
            source = jnp.maximum(back_ref[place + 1], 0)
            lifted = mm(got[k][c], mine_ref[source]).astype(BF16)
            behind_ref[k, c] = mm(peers[k][target], lifted, TN).astype(BF16)


def far_call(slots, back, bases, blocks, peer_bases, peer_blocks):
    neigh, cap = blocks.shape[0], blocks.shape[1]
    width = bases.shape[2]
    shape = jax.ShapeDtypeStruct((neigh, cap, width, width), BF16)

    def kernel(*refs):
        far_kernel(neigh, cap, *refs)

    return pl.pallas_call(
        kernel,
        out_shape=(shape, shape),
        in_specs=[smem(), smem()] + [vmem()] * (2 + 2 * neigh),
        out_specs=(vmem(), vmem()),
        compiler_params=params(),
        cost_estimate=pl.CostEstimate(flops=10**8, bytes_accessed=4 * 10**6, transcendentals=0),
        name="far_blocks",
    )(slots, back, bases, blocks, *peer_bases, *peer_blocks)


def join_kernel(
    neigh, near_ref, nback_ref, far_ref, fback_ref, local_ref, v_ref, w_ref, u_ref,
    blocks_ref, ahead_ref, behind_ref, *refs
):
    fields, got = refs[:neigh], refs[neigh : 2 * neigh]
    out_ref, next_ref, acc_a, acc_b = refs[2 * neigh :]
    leaves, rows, width = local_ref.shape
    acc_a[:leaves] = local_ref[...]
    acc_b[...] = jnp.zeros_like(acc_b)
    near_cap, far_cap = blocks_ref.shape[1], ahead_ref.shape[1]

    def parent(e, total):
        return total + mm(u_ref[e], w_ref[e])

    total = lax.fori_loop(0, u_ref.shape[0], parent, jnp.zeros(next_ref.shape, F32))
    down = total.astype(BF16)

    for k in range(neigh):
        work = []
        for c in range(near_cap + far_cap):
            if c < near_cap:
                go, back, place = near_ref, nback_ref, (k * near_cap + c) * 2
                ahead, behind, dims = blocks_ref[k, c], got[k][c], NT
            else:
                go, back, place = far_ref, fback_ref, (k * far_cap + c - near_cap) * 2
                ahead, behind, dims = ahead_ref[k, c - near_cap], behind_ref[k, c - near_cap], NN
            target, source = go[place], go[place + 1]
            there, here = back[place], back[place + 1]
            work.append(
                (
                    jnp.where(target < 0, leaves, target),
                    jnp.where(here < 0, leaves, here),
                    mm(leaf_cols(fields[k], jnp.maximum(source, 0), width), ahead),
                    mm(leaf_cols(fields[k], jnp.maximum(there, 0), width), behind, dims),
                )
            )
        for target, here, one, two in work:
            acc_a[target] += one
            acc_b[here] += two
    for leaf in range(leaves):
        cols = slice(leaf * width, (leaf + 1) * width)
        out_ref[:, cols] = (acc_a[leaf] + acc_b[leaf] + mm(down, v_ref[:, cols])).astype(BF16)
    next_ref[...] = mm(out_ref[...], v_ref[...], NT).astype(BF16)


def join_call(tables, local_sum, v, w, u_all, blocks, far, fields, got):
    neigh = blocks.shape[0]
    leaves, rows, width = local_sum.shape

    def kernel(*refs):
        join_kernel(neigh, *refs)

    return pl.pallas_call(
        kernel,
        out_shape=(
            jax.ShapeDtypeStruct((rows, leaves * width), BF16),
            jax.ShapeDtypeStruct((rows, v.shape[0]), BF16),
        ),
        in_specs=[smem()] * 4 + [vmem()] * (7 + 2 * neigh),
        out_specs=(vmem(), vmem()),
        scratch_shapes=[pltpu.VMEM((leaves + 1, rows, width), F32)] * 2,
        compiler_params=params(),
        cost_estimate=pl.CostEstimate(flops=10**9, bytes_accessed=8 * 10**6, transcendentals=0),
        name="near_and_join",
    )(*tables, local_sum, v, w, u_all, blocks, *far, *fields, *got)


def body(
    rhs,
    bases,
    transfers,
    near_slots,
    near_blocks,
    local_pairs,
    local_blocks,
    far_slots,
    far_blocks,
    parent_pairs,
    parent_blocks,
):
    neigh = near_slots.shape[1]
    offsets = neighbour_offsets(neigh)
    near, far = near_blocks[0], far_blocks[0]
    near_cap, far_cap = near.shape[1], far.shape[1]

    def send(pick):
        return [shifted(pick(neigh - 1 - k), "leaf", -offsets[k]) for k in range(neigh)]

    fields = send(lambda k: rhs)
    slots = jnp.concatenate([near_slots[0], far_slots[0]], axis=1)
    back = jnp.stack(send(lambda k: slots[k]))
    got_bases = send(lambda k: bases)
    got_far = send(lambda k: far[k])
    got_near = send(lambda k: near[k])
    tables = [
        near_slots.reshape(-1),
        back[:, :near_cap].reshape(-1),
        far_slots.reshape(-1),
        back[:, near_cap:].reshape(-1),
    ]

    v, u = start_call(rhs, bases, transfers)

    owners = lax.axis_size("leaf")
    me = lax.axis_index("leaf")
    all_blocks = lax.all_gather(parent_blocks[0], "leaf", axis=0)
    all_pairs = lax.all_gather(parent_pairs[0], "leaf", axis=0)
    ids = jnp.arange(owners, dtype=jnp.int32)
    mine = (parent_pairs[0][:, None] == ids[None, :]).astype(F32)
    theirs = (all_pairs == me).astype(F32)
    w = jnp.sum(
        mine[:, :, None, None] * parent_blocks[0].astype(F32).transpose(0, 2, 1)[:, None], axis=0
    ) + jnp.sum(theirs[:, :, None, None] * all_blocks.astype(F32), axis=1)
    w = w.astype(BF16)

    u_all = lax.all_gather(u, "leaf", axis=0)
    local_sum = local_call(rhs, local_pairs[0], local_blocks[0])
    effective = far_call(tables[2], tables[3], bases, far, got_bases, got_far)
    first, u = join_call(tables, local_sum, v, w, u_all, near, effective, fields, got_near)

    fields = send(lambda k: first)
    u_all = lax.all_gather(u, "leaf", axis=0)
    local_sum = local_call(first, local_pairs[0], local_blocks[0])
    second, _ = join_call(tables, local_sum, v, w, u_all, near, effective, fields, got_near)
    return (first, second)


def solution(mesh):
    in_specs = (
        P("groups", "leaf"),
        P(("groups", "leaf"), None, None),
        P(("groups", "leaf"), None, None),
        P(("groups", "leaf"), None, None, None),
        P(("groups", "leaf"), None, None, None, None),
        P(("groups", "leaf"), None, None),
        P(("groups", "leaf"), None, None, None),
        P(("groups", "leaf"), None, None, None),
        P(("groups", "leaf"), None, None, None, None),
        P(("groups", "leaf"), None),
        P(("groups", "leaf"), None, None, None),
    )
    out_specs = (P("groups", "leaf"), P("groups", "leaf"))
    return jax.shard_map(body, mesh=mesh, in_specs=in_specs, out_specs=out_specs, check_vma=False)
```

time: 471 us -> 338 us (0.72)
  waiting for transfers between devices: 136 us -> 7.3 us
  matrix products: 81.2 us -> 0 us
  blocking collectives: 35.8 us -> 87.3 us
  Pallas kernels: 0 us -> 41 us
  between operations: 15.9 us -> 1.78 us
  other arithmetic: 6.22 us -> 1.36 us
    ppermute x56 -> x48, waiting for transfers between devices: 136 us -> 7.3 us  [shifted(): return lax.ppermute(shard, axis, pairs)]
    dot_general x38 -> x0, matrix products: 81.2 us -> none  [the longest x14 35.8 us: spread_rows(): jnp.einsum('jl,j...->l...', onehot, flat_values, precision=lax.Precision....]
    all_gather x2 -> x4, blocking collectives: 35.8 us -> 87.3 us  [the longest x2 48 us: body(): u_all = lax.all_gather(u, 'leaf', axis=0)]
    pallas_call x0 -> x6, Pallas kernels: none -> 41 us  [the longest x2 25.6 us: local_call(): pl.pallas_call(kernel, grid=(steps,), out_shape=jax.ShapeDtypeStruct(shap...]
    unnamed x185 -> x173, local copies, waits for them, and re-layouts: 19.9 us -> 58.3 us
    gather x19 -> x0, local copies, waits for them, and re-layouts: 27.5 us -> none  [pick_rows(): picked = jnp.take(source_table, safe_index, axis=0)]
    ppermute x56 -> x48, starting transfers between devices: 121 us -> 125 us  [shifted(): return lax.ppermute(shard, axis, pairs)]
  transfers between devices with their start and end apart: 58 -> 48, of which waited for: 43 -> 6; matrix products, arithmetic and copies ran while one was open for 21% -> 6% of each run, Pallas kernels for 0% -> 9%
where the time goes in v1:
time: 338 us; the launch traced here: 335 us
  starting transfers between devices  125 us (37%)
  blocking collectives  87.3 us (26%)
  local copies, waits for them, and re-layouts  71.3 us (21%)
  Pallas kernels  41 us (12%)
  waiting for transfers between devices  7.3 us (2%)
    ppermute x48, starting transfers between devices, shifted(): return lax.ppermute(shard, axis, pairs)  125 us
    unnamed x173, local copies, waits for them, and re-layouts  58.3 us
    all_gather x2, blocking collectives, body(): u_all = lax.all_gather(u, 'leaf', axis=0)  48 us
    pallas_call x2, Pallas kernels, local_call(): pl.pallas_call(kernel, grid=(steps,), out_shape=jax.ShapeDtypeStruct(shap...  25.6 us
    all_gather x1, blocking collectives, body(): all_blocks = lax.all_gather(parent_blocks[0], 'leaf', axis=0)  21.9 us
    all_gather x1, blocking collectives, body(): all_pairs = lax.all_gather(parent_pairs[0], 'leaf', axis=0)  17.3 us
    pallas_call x2, Pallas kernels, join_call(): pl.pallas_call(kernel, out_shape=(jax.ShapeDtypeStruct((rows, leaves * wi...  12.2 us
    ppermute x48, waiting for transfers between devices, shifted(): return lax.ppermute(shard, axis, pairs)  7.3 us
  transfers between devices with their start and end apart: 48, of which 6 were waited for; matrix products, arithmetic and copies ran while one was open for 6% of the time, Pallas kernels for 9%

profile of v1, /device:TPU:0, one launch (start us, length us, event | category | flops | bytes accessed | tf_op | source)
XLA Modules:
  0.0 335.4 jit_solution(6137895745600322688)
XLA Ops:
  2.2 4.9 %collective-permute-start = (s32[10,2]{0,1:T(2,128)S(1)}, s32[10,2]{0,1:T(2,128)S(1)}, u32[]{:S(2)}, u32[]{:S(2)}) collective-permute-start(s32[10,2]{0,1:T(2,128)S(1)} %bitcast.96), channel_id=1, source_target_pairs={{0,4},{1,5},{2,6},{3,7},{4,8},{5,9},{6,10},{7,11},{8,12},{9,13},{1... | collective-permute-start | bytes 248 | tf_op jit(solution)/shard_map/ppermute | solution.py:22
  7.1 2.6 collective-permute-start.1
  9.7 3.5 %collective-permute-start.2 = (s32[10,2]{0,1:T(2,128)S(1)}, s32[10,2]{0,1:T(2,128)S(1)}, u32[]{:S(2)}, u32[]{:S(2)}) collective-permute-start(s32[10,2]{0,1:T(2,128)S(1)} %bitcast.94), channel_id=1, source_target_pairs={{0,2},{1,3},{2,4},{3,5},{4,6},{5,7},{6,8},{7,9},{8,10},{9,11},{10,... | collective-permute-start | bytes 248 | tf_op jit(solution)/shard_map/ppermute | solution.py:22
  13.2 2.6 collective-permute-start.3
  15.8 1.3 collective-permute-start.4
  17.8 21.9 %all_gather.19 = bf16[16,4,32,32]{3,2,1,0:T(8,128)(2,1)S(1)} all-gather(bf16[1,4,32,32]{3,2,1,0:T(8,128)(2,1)} %param.21), channel_id=1, replica_groups=mesh['groups'=2,'leaf'=16] {'leaf'}, dimensions={0}, use_global_device_ids=true | all-gather | bytes 139264 | tf_op jit(solution)/shard_map/all_gather | solution.py:280
  41.3 1.5 slice_bitcast_fusion.8
  43.4 2.9 slice_bitcast_fusion
  46.6 17.3 %all-gather.2 = s32[16,1,4]{2,1,0:T(1,128)S(1)} all-gather(s32[1,1,4]{2,1,0:T(1,128)S(1)} %bitcast.87), channel_id=1, replica_groups=mesh['groups'=2,'leaf'=16] {'leaf'}, dimensions={0}, use_global_device_ids=true | all-gather | bytes 272 | tf_op jit(solution)/shard_map/all_gather | solution.py:281
  65.3 20.5 %all-gather = bf16[512,32]{1,0:T(8,128)(2,1)} all-gather(bf16[32,32]{1,0:T(8,128)(2,1)S(1)} %get-tuple-element.10), channel_id=2, replica_groups=mesh['groups'=2,'leaf'=16] {'leaf'}, dimensions={0}, use_global_device_ids=true | all-gather | bytes 34816 | tf_op jit(solution)/shard_map/all_gather | solution.py:290
  85.8 3.7 %copy-done.70 = bf16[1,288,128,128]{3,2,1,0:T(8,128)(2,1)S(1)} copy-done((bf16[1,288,128,128]{3,2,1,0:T(8,128)(2,1)S(1)}, bf16[1,288,128,128]{3,2,1,0:T(8,128)(2,1)}, u32[]{:S(2)}) %copy-start.70) | copy-done | bytes 9437208
  89.5 12.8 %local_blocks.2.refs_4_ = f32[16,32,128]{2,1,0:T(8,128)S(1)} custom-call(s32[576]{0:T(1024)S(1)} %reshape_squeeze.4.refs_0_, bf16[32,2048]{1,0:T(8,128)(2,1)S(1)} %copy-done.11, bf16[288,128,128]{2,1,0:T(8,128)(2,1)S(1)} %bitcast.82), custom_call_target="tpu_custom_call" | custom-call | flops 9663676416 | bytes 9437184 | tf_op jit(solution)/shard_map/local_blocks/pallas_call | solution.py:119
  105.2 1.3 collective-permute-start.6
  106.5 1.3 collective-permute-start.7
  107.8 5.6 %collective-permute-start.16 = (bf16[2,32,32]{2,1,0:T(8,128)(2,1)}, bf16[2,32,32]{2,1,0:T(8,128)(2,1)S(1)}, u32[]{:S(2)}, u32[]{:S(2)}) collective-permute-start(bf16[2,32,32]{2,1,0:T(8,128)(2,1)} %get-tuple-element.30), channel_id=1, source_target_pairs={{0,4},{1,5},{2,6},{3,7},{4,8},{5,9},{6,10},{7,11},{8,12},{9,13},{1... | collective-permute-start | bytes 12296 | tf_op jit(solution)/shard_map/ppermute | solution.py:22
  113.5 3.4 %collective-permute-start.17 = (bf16[2,32,32]{2,1,0:T(8,128)(2,1)}, bf16[2,32,32]{2,1,0:T(8,128)(2,1)S(1)}, u32[]{:S(2)}, u32[]{:S(2)}) collective-permute-start(bf16[2,32,32]{2,1,0:T(8,128)(2,1)} %get-tuple-element.29), channel_id=1, source_target_pairs={{0,3},{1,4},{2,5},{3,6},{4,7},{5,8},{6,9},{7,10},{8,11},{9,12},{10... | collective-permute-start | bytes 12296 | tf_op jit(solution)/shard_map/ppermute | solution.py:22
  116.9 4.8 %collective-permute-start.18 = (bf16[2,32,32]{2,1,0:T(8,128)(2,1)}, bf16[2,32,32]{2,1,0:T(8,128)(2,1)S(1)}, u32[]{:S(2)}, u32[]{:S(2)}) collective-permute-start(bf16[2,32,32]{2,1,0:T(8,128)(2,1)} %get-tuple-element.28), channel_id=1, source_target_pairs={{0,2},{1,3},{2,4},{3,5},{4,6},{5,7},{6,8},{7,9},{8,10},{9,11},{10,... | collective-permute-start | bytes 12296 | tf_op jit(solution)/shard_map/ppermute | solution.py:22
  121.7 1.4 collective-permute-start.19
  123.0 1.3 collective-permute-start.20
  125.0 5.2 %collective-permute-start.10 = (bf16[16,32,128]{2,1,0:T(8,128)(2,1)S(1)}, bf16[16,32,128]{2,1,0:T(8,128)(2,1)S(1)}, u32[]{:S(2)}, u32[]{:S(2)}) collective-permute-start(bf16[16,32,128]{2,1,0:T(8,128)(2,1)S(1)} %copy-done.1), channel_id=1, source_target_pairs={{0,2},{1,3},{2,4},{3,5},{4,6},{5,7},{6,8},{7,9},{8,10},{9,11},{10,... | collective-permute-start | bytes 393224 | tf_op jit(solution)/shard_map/ppermute | solution.py:22
  130.8 1.4 collective-permute-start.11
  141.1 1.8 collective-permute-done.22.refs_18_
  150.3 8.0 %collective-permute-start.8 = (bf16[16,32,128]{2,1,0:T(8,128)(2,1)S(1)}, bf16[16,32,128]{2,1,0:T(8,128)(2,1)S(1)}, u32[]{:S(2)}, u32[]{:S(2)}) collective-permute-start(bf16[16,32,128]{2,1,0:T(8,128)(2,1)S(1)} %copy-done.1), channel_id=1, source_target_pairs={{0,4},{1,5},{2,6},{3,7},{4,8},{5,9},{6,10},{7,11},{8,12},{9,13},{1... | collective-permute-start | bytes 393224 | tf_op jit(solution)/shard_map/ppermute | solution.py:22
  159.6 3.4 collective-permute-start.9
  163.7 4.5 %collective-permute-start.24 = (bf16[32,2048]{1,0:T(8,128)(2,1)S(1)}, bf16[32,2048]{1,0:T(8,128)(2,1)S(1)}, u32[]{:S(2)}, u32[]{:S(2)}) collective-permute-start(bf16[32,2048]{1,0:T(8,128)(2,1)S(1)} %copy-done.11), channel_id=1, source_target_pairs={{0,4},{1,5},{2,6},{3,7},{4,8},{5,9},{6,10},{7,11},{8,12},{9,13},{1... | collective-permute-start | bytes 393224 | tf_op jit(solution)/shard_map/ppermute | solution.py:22
  168.9 3.7 %collective-permute-start.25 = (bf16[32,2048]{1,0:T(8,128)(2,1)S(1)}, bf16[32,2048]{1,0:T(8,128)(2,1)S(1)}, u32[]{:S(2)}, u32[]{:S(2)}) collective-permute-start(bf16[32,2048]{1,0:T(8,128)(2,1)S(1)} %copy-done.11), channel_id=1, source_target_pairs={{0,3},{1,4},{2,5},{3,6},{4,7},{5,8},{6,9},{7,10},{8,11},{9,12},{10... | collective-permute-start | bytes 393224 | tf_op jit(solution)/shard_map/ppermute | solution.py:22
  173.2 1.9 collective-permute-start.26
  175.8 2.3 collective-permute-start.27
  183.3 7.7 %collective-permute-start.32 = (bf16[8,128,128]{2,1,0:T(8,128)(2,1)}, bf16[8,128,128]{2,1,0:T(8,128)(2,1)S(1)}, u32[]{:S(2)}, u32[]{:S(2)}) collective-permute-start(bf16[8,128,128]{2,1,0:T(8,128)(2,1)} %get-tuple-element.22), channel_id=1, source_target_pairs={{0,4},{1,5},{2,6},{3,7},{4,8},{5,9},{6,10},{7,11},{8,12},{9,13},{1... | collective-permute-start | bytes 786440 | tf_op jit(solution)/shard_map/ppermute | solution.py:22
  191.7 1.3 collective-permute-start.33
  193.6 2.2 collective-permute-start.34
  200.4 3.0 collective-permute-done.30.refs_17_
  204.1 3.2 collective-permute-start.35
  215.1 1.4 copy.57
  216.5 1.4 reshape.80.refs_1_.refs_3_
  217.9 1.4 copy.55
  219.3 1.4 reshape.78.refs_1_
  236.1 2.9 far_blocks.1
  251.7 6.0 %near_and_join.2 = (bf16[32,2048]{1,0:T(8,128)(2,1)}, bf16[32,32]{1,0:T(8,128)(2,1)S(1)}) custom-call(s32[128]{0:T(128)S(1)} %copy-done.64, s32[128]{0:T(128)S(1)} %copy-done.66, s32[32]{0:T(128)S(1)} %copy-done.59, s32[32]{0:T(128)S(1)} %copy-done.62, f32[16,32,128]{2,1,0:T(8,128)S(1)} %copy-done.9, bf16[32,2048]{1,0:T(8,128)(2,1)S(1)} %copy-done.4, ...), custom_call_target="tpu_custom_call" | custom-call | flops 1000000000 | bytes 8000000 | tf_op jit(solution)/shard_map/near_and_join/pallas_call | solution.py:227
  257.8 11.6 %collective-permute-start.40 = (bf16[32,2048]{1,0:T(8,128)(2,1)}, bf16[32,2048]{1,0:T(8,128)(2,1)S(1)}, u32[]{:S(2)}, u32[]{:S(2)}) collective-permute-start(bf16[32,2048]{1,0:T(8,128)(2,1)} %get-tuple-element.7.refs_1_), channel_id=1, source_target_pairs={{0,4},{1,5},{2,6},{3,7},{4,8},{5,9},{6,10},{7,11},{8,12},{9,13},{1... | collective-permute-start | bytes 393224 | tf_op jit(solution)/shard_map/ppermute | solution.py:22
  269.4 3.4 %collective-permute-start.41 = (bf16[32,2048]{1,0:T(8,128)(2,1)}, bf16[32,2048]{1,0:T(8,128)(2,1)S(1)}, u32[]{:S(2)}, u32[]{:S(2)}) collective-permute-start(bf16[32,2048]{1,0:T(8,128)(2,1)} %get-tuple-element.7.refs_1_), channel_id=1, source_target_pairs={{0,3},{1,4},{2,5},{3,6},{4,7},{5,8},{6,9},{7,10},{8,11},{9,12},{10... | collective-permute-start | bytes 393224 | tf_op jit(solution)/shard_map/ppermute | solution.py:22
  272.8 4.8 %collective-permute-start.42 = (bf16[32,2048]{1,0:T(8,128)(2,1)}, bf16[32,2048]{1,0:T(8,128)(2,1)S(1)}, u32[]{:S(2)}, u32[]{:S(2)}) collective-permute-start(bf16[32,2048]{1,0:T(8,128)(2,1)} %get-tuple-element.7.refs_1_), channel_id=1, source_target_pairs={{0,2},{1,3},{2,4},{3,5},{4,6},{5,7},{6,8},{7,9},{8,10},{9,11},{10,... | collective-permute-start | bytes 393224 | tf_op jit(solution)/shard_map/ppermute | solution.py:22
  277.6 1.4 collective-permute-start.43
  281.6 1.3 collective-permute-start.46
  284.3 3.7 %copy-done.71 = bf16[1,288,128,128]{3,2,1,0:T(8,128)(2,1)S(1)} copy-done((bf16[1,288,128,128]{3,2,1,0:T(8,128)(2,1)S(1)}, bf16[1,288,128,128]{3,2,1,0:T(8,128)(2,1)}, u32[]{:S(2)}) %copy-start.71) | copy-done | bytes 9437208
  288.8 12.8 %local_blocks.3.refs_4_ = f32[16,32,128]{2,1,0:T(8,128)S(1)} custom-call(s32[576]{0:T(1024)S(1)} %copy-done.69, bf16[32,2048]{1,0:T(8,128)(2,1)S(1)} %copy-done.72, bf16[288,128,128]{2,1,0:T(8,128)(2,1)S(1)} %bitcast.83), custom_call_target="tpu_custom_call" | custom-call | flops 9663676416 | bytes 9437184 | tf_op jit(solution)/shard_map/local_blocks/pallas_call | solution.py:119
  301.6 27.5 %all-gather.1 = bf16[512,32]{1,0:T(8,128)(2,1)S(1)} all-gather(bf16[32,32]{1,0:T(8,128)(2,1)S(1)} %get-tuple-element.14), channel_id=3, replica_groups=mesh['groups'=2,'leaf'=16] {'leaf'}, dimensions={0}, use_global_device_ids=true | all-gather | bytes 34816 | tf_op jit(solution)/shard_map/all_gather | solution.py:296
  329.2 6.2 %near_and_join.3 = (bf16[32,2048]{1,0:T(8,128)(2,1)}, bf16[32,32]{1,0:T(8,128)(2,1)}) custom-call(s32[128]{0:T(128)S(1)} %copy-done.65, s32[128]{0:T(128)S(1)} %copy-done.67, s32[32]{0:T(128)S(1)} %copy-done.60, s32[32]{0:T(128)S(1)} %copy-done.63, f32[16,32,128]{2,1,0:T(8,128)S(1)} %local_blocks.3.refs_4_, bf16[32,2048]{1,0:T(8,128)(2,1)S(1)} %copy-done.5, ...), custom_call_target="tpu_custom_call" | custom-call | flops 1000000000 | bytes 8000000 | tf_op jit(solution)/shard_map/near_and_join/pallas_call | solution.py:227
  (253 shorter events, 82.6 us)
Async XLA Ops:
  2.2 101.7 %collective-permute-start = (s32[10,2]{0,1:T(2,128)S(1)}, s32[10,2]{0,1:T(2,128)S(1)}, u32[]{:S(2)}, u32[]{:S(2)}) collective-permute-start(s32[10,2]{0,1:T(2,128)S(1)} %bitcast.96), channel_id=1, source_target_pairs={{0,4},{1,5},{2,6},{3,7},{4,8},{5,9},{6,10},{7,11},{8,12},{9,13},{1... | collective-permute-start | bytes 248 | tf_op jit(solution)/shard_map/ppermute | solution.py:22
  7.1 98.1 %collective-permute-start.1 = (s32[10,2]{0,1:T(2,128)S(1)}, s32[10,2]{0,1:T(2,128)S(1)}, u32[]{:S(2)}, u32[]{:S(2)}) collective-permute-start(s32[10,2]{0,1:T(2,128)S(1)} %bitcast.95), channel_id=1, source_target_pairs={{0,3},{1,4},{2,5},{3,6},{4,7},{5,8},{6,9},{7,10},{8,11},{9,12},{10... | collective-permute-start | bytes 248 | tf_op jit(solution)/shard_map/ppermute | solution.py:22
  9.7 96.8 %collective-permute-start.2 = (s32[10,2]{0,1:T(2,128)S(1)}, s32[10,2]{0,1:T(2,128)S(1)}, u32[]{:S(2)}, u32[]{:S(2)}) collective-permute-start(s32[10,2]{0,1:T(2,128)S(1)} %bitcast.94), channel_id=1, source_target_pairs={{0,2},{1,3},{2,4},{3,5},{4,6},{5,7},{6,8},{7,9},{8,10},{9,11},{10,... | collective-permute-start | bytes 248 | tf_op jit(solution)/shard_map/ppermute | solution.py:22
  13.2 94.7 %collective-permute-start.3 = (s32[10,2]{0,1:T(2,128)S(1)}, s32[10,2]{0,1:T(2,128)S(1)}, u32[]{:S(2)}, u32[]{:S(2)}) collective-permute-start(s32[10,2]{0,1:T(2,128)S(1)} %bitcast.93), channel_id=1, source_target_pairs={{0,1},{1,2},{2,3},{3,4},{4,5},{5,6},{6,7},{7,8},{8,9},{9,10},{10,1... | collective-permute-start | bytes 248 | tf_op jit(solution)/shard_map/ppermute | solution.py:22
  15.8 97.7 %collective-permute-start.4 = (s32[10,2]{0,1:T(2,128)S(1)}, s32[10,2]{0,1:T(2,128)S(1)}, u32[]{:S(2)}, u32[]{:S(2)}) collective-permute-start(s32[10,2]{0,1:T(2,128)S(1)} %bitcast.92), channel_id=1, source_target_pairs={{1,0},{2,1},{3,2},{4,3},{5,4},{6,5},{7,6},{8,7},{9,8},{10,9},{11,1... | collective-permute-start | bytes 248 | tf_op jit(solution)/shard_map/ppermute | solution.py:22
  103.9 12.9 %collective-permute-start.5 = (s32[10,2]{0,1:T(2,128)S(1)}, s32[10,2]{0,1:T(2,128)S(1)}, u32[]{:S(2)}, u32[]{:S(2)}) collective-permute-start(s32[10,2]{0,1:T(2,128)S(1)} %bitcast.91), channel_id=1, source_target_pairs={{2,0},{3,1},{4,2},{5,3},{6,4},{7,5},{8,6},{9,7},{10,8},{11,9},{12,... | collective-permute-start | bytes 248 | tf_op jit(solution)/shard_map/ppermute | solution.py:22
  105.2 16.4 %collective-permute-start.6 = (s32[10,2]{0,1:T(2,128)S(1)}, s32[10,2]{0,1:T(2,128)S(1)}, u32[]{:S(2)}, u32[]{:S(2)}) collective-permute-start(s32[10,2]{0,1:T(2,128)S(1)} %bitcast.90), channel_id=1, source_target_pairs={{3,0},{4,1},{5,2},{6,3},{7,4},{8,5},{9,6},{10,7},{11,8},{12,9},{13... | collective-permute-start | bytes 248 | tf_op jit(solution)/shard_map/ppermute | solution.py:22
  106.5 16.5 %collective-permute-start.7 = (s32[10,2]{0,1:T(2,128)S(1)}, s32[10,2]{0,1:T(2,128)S(1)}, u32[]{:S(2)}, u32[]{:S(2)}) collective-permute-start(s32[10,2]{0,1:T(2,128)S(1)} %bitcast.89), channel_id=1, source_target_pairs={{4,0},{5,1},{6,2},{7,3},{8,4},{9,5},{10,6},{11,7},{12,8},{13,9},{1... | collective-permute-start | bytes 248 | tf_op jit(solution)/shard_map/ppermute | solution.py:22
  107.8 17.2 %collective-permute-start.16 = (bf16[2,32,32]{2,1,0:T(8,128)(2,1)}, bf16[2,32,32]{2,1,0:T(8,128)(2,1)S(1)}, u32[]{:S(2)}, u32[]{:S(2)}) collective-permute-start(bf16[2,32,32]{2,1,0:T(8,128)(2,1)} %get-tuple-element.30), channel_id=1, source_target_pairs={{0,4},{1,5},{2,6},{3,7},{4,8},{5,9},{6,10},{7,11},{8,12},{9,13},{1... | collective-permute-start | bytes 12296 | tf_op jit(solution)/shard_map/ppermute | solution.py:22
  113.5 16.7 %collective-permute-start.17 = (bf16[2,32,32]{2,1,0:T(8,128)(2,1)}, bf16[2,32,32]{2,1,0:T(8,128)(2,1)S(1)}, u32[]{:S(2)}, u32[]{:S(2)}) collective-permute-start(bf16[2,32,32]{2,1,0:T(8,128)(2,1)} %get-tuple-element.29), channel_id=1, source_target_pairs={{0,3},{1,4},{2,5},{3,6},{4,7},{5,8},{6,9},{7,10},{8,11},{9,12},{10... | collective-permute-start | bytes 12296 | tf_op jit(solution)/shard_map/ppermute | solution.py:22
  116.9 15.4 %collective-permute-start.18 = (bf16[2,32,32]{2,1,0:T(8,128)(2,1)}, bf16[2,32,32]{2,1,0:T(8,128)(2,1)S(1)}, u32[]{:S(2)}, u32[]{:S(2)}) collective-permute-start(bf16[2,32,32]{2,1,0:T(8,128)(2,1)} %get-tuple-element.28), channel_id=1, source_target_pairs={{0,2},{1,3},{2,4},{3,5},{4,6},{5,7},{6,8},{7,9},{8,10},{9,11},{10,... | collective-permute-start | bytes 12296 | tf_op jit(solution)/shard_map/ppermute | solution.py:22
  121.7 12.5 %collective-permute-start.19 = (bf16[2,32,32]{2,1,0:T(8,128)(2,1)S(1)}, bf16[2,32,32]{2,1,0:T(8,128)(2,1)S(1)}, u32[]{:S(2)}, u32[]{:S(2)}) collective-permute-start(bf16[2,32,32]{2,1,0:T(8,128)(2,1)S(1)} %get-tuple-element.27), channel_id=1, source_target_pairs={{0,1},{1,2},{2,3},{3,4},{4,5},{5,6},{6,7},{7,8},{8,9},{9,10},{10,1... | collective-permute-start | bytes 12296 | tf_op jit(solution)/shard_map/ppermute | solution.py:22
  123.0 13.0 %collective-permute-start.20 = (bf16[2,32,32]{2,1,0:T(8,128)(2,1)S(1)}, bf16[2,32,32]{2,1,0:T(8,128)(2,1)S(1)}, u32[]{:S(2)}, u32[]{:S(2)}) collective-permute-start(bf16[2,32,32]{2,1,0:T(8,128)(2,1)S(1)} %get-tuple-element.26), channel_id=1, source_target_pairs={{1,0},{2,1},{3,2},{4,3},{5,4},{6,5},{7,6},{8,7},{9,8},{10,9},{11,1... | collective-permute-start | bytes 12296 | tf_op jit(solution)/shard_map/ppermute | solution.py:22
  125.0 22.6 %collective-permute-start.10 = (bf16[16,32,128]{2,1,0:T(8,128)(2,1)S(1)}, bf16[16,32,128]{2,1,0:T(8,128)(2,1)S(1)}, u32[]{:S(2)}, u32[]{:S(2)}) collective-permute-start(bf16[16,32,128]{2,1,0:T(8,128)(2,1)S(1)} %copy-done.1), channel_id=1, source_target_pairs={{0,2},{1,3},{2,4},{3,5},{4,6},{5,7},{6,8},{7,9},{8,10},{9,11},{10,... | collective-permute-start | bytes 393224 | tf_op jit(solution)/shard_map/ppermute | solution.py:22
  130.8 18.8 %collective-permute-start.11 = (bf16[16,32,128]{2,1,0:T(8,128)(2,1)S(1)}, bf16[16,32,128]{2,1,0:T(8,128)(2,1)S(1)}, u32[]{:S(2)}, u32[]{:S(2)}) collective-permute-start(bf16[16,32,128]{2,1,0:T(8,128)(2,1)S(1)} %copy-done.1), channel_id=1, source_target_pairs={{0,1},{1,2},{2,3},{3,4},{4,5},{5,6},{6,7},{7,8},{8,9},{9,10},{10,1... | collective-permute-start | bytes 393224 | tf_op jit(solution)/shard_map/ppermute | solution.py:22
  132.8 6.4 %collective-permute-start.21 = (bf16[2,32,32]{2,1,0:T(8,128)(2,1)S(1)}, bf16[2,32,32]{2,1,0:T(8,128)(2,1)S(1)}, u32[]{:S(2)}, u32[]{:S(2)}) collective-permute-start(bf16[2,32,32]{2,1,0:T(8,128)(2,1)S(1)} %get-tuple-element.25), channel_id=1, source_target_pairs={{2,0},{3,1},{4,2},{5,3},{6,4},{7,5},{8,6},{9,7},{10,8},{11,9},{12,... | collective-permute-start | bytes 12296 | tf_op jit(solution)/shard_map/ppermute | solution.py:22
  134.7 8.2 %collective-permute-start.22 = (bf16[2,32,32]{2,1,0:T(8,128)(2,1)S(1)}, bf16[2,32,32]{2,1,0:T(8,128)(2,1)S(1)}, u32[]{:S(2)}, u32[]{:S(2)}) collective-permute-start(bf16[2,32,32]{2,1,0:T(8,128)(2,1)S(1)} %get-tuple-element.31), channel_id=1, source_target_pairs={{3,0},{4,1},{5,2},{6,3},{7,4},{8,5},{9,6},{10,7},{11,8},{12,9},{13... | collective-permute-start | bytes 12296 | tf_op jit(solution)/shard_map/ppermute | solution.py:22
  136.6 9.1 %collective-permute-start.23 = (bf16[2,32,32]{2,1,0:T(8,128)(2,1)S(1)}, bf16[2,32,32]{2,1,0:T(8,128)(2,1)S(1)}, u32[]{:S(2)}, u32[]{:S(2)}) collective-permute-start(bf16[2,32,32]{2,1,0:T(8,128)(2,1)S(1)} %get-tuple-element.24), channel_id=1, source_target_pairs={{4,0},{5,1},{6,2},{7,3},{8,4},{9,5},{10,6},{11,7},{12,8},{13,9},{1... | collective-permute-start | bytes 12296 | tf_op jit(solution)/shard_map/ppermute | solution.py:22
  139.8 19.1 %collective-permute-start.12 = (bf16[16,32,128]{2,1,0:T(8,128)(2,1)S(1)}, bf16[16,32,128]{2,1,0:T(8,128)(2,1)S(1)}, u32[]{:S(2)}, u32[]{:S(2)}) collective-permute-start(bf16[16,32,128]{2,1,0:T(8,128)(2,1)S(1)} %copy-done.1), channel_id=1, source_target_pairs={{1,0},{2,1},{3,2},{4,3},{5,4},{6,5},{7,6},{8,7},{9,8},{10,9},{11,1... | collective-permute-start | bytes 393224 | tf_op jit(solution)/shard_map/ppermute | solution.py:22
  143.5 19.5 %collective-permute-start.13 = (bf16[16,32,128]{2,1,0:T(8,128)(2,1)S(1)}, bf16[16,32,128]{2,1,0:T(8,128)(2,1)S(1)}, u32[]{:S(2)}, u32[]{:S(2)}) collective-permute-start(bf16[16,32,128]{2,1,0:T(8,128)(2,1)S(1)} %copy-done.1), channel_id=1, source_target_pairs={{2,0},{3,1},{4,2},{5,3},{6,4},{7,5},{8,6},{9,7},{10,8},{11,9},{12,... | collective-permute-start | bytes 393224 | tf_op jit(solution)/shard_map/ppermute | solution.py:22
  146.3 21.9 %collective-permute-start.14 = (bf16[16,32,128]{2,1,0:T(8,128)(2,1)S(1)}, bf16[16,32,128]{2,1,0:T(8,128)(2,1)S(1)}, u32[]{:S(2)}, u32[]{:S(2)}) collective-permute-start(bf16[16,32,128]{2,1,0:T(8,128)(2,1)S(1)} %copy-done.1), channel_id=1, source_target_pairs={{3,0},{4,1},{5,2},{6,3},{7,4},{8,5},{9,6},{10,7},{11,8},{12,9},{13... | collective-permute-start | bytes 393224 | tf_op jit(solution)/shard_map/ppermute | solution.py:22
  148.3 24.3 %collective-permute-start.15 = (bf16[16,32,128]{2,1,0:T(8,128)(2,1)S(1)}, bf16[16,32,128]{2,1,0:T(8,128)(2,1)S(1)}, u32[]{:S(2)}, u32[]{:S(2)}) collective-permute-start(bf16[16,32,128]{2,1,0:T(8,128)(2,1)S(1)} %copy-done.1), channel_id=1, source_target_pairs={{4,0},{5,1},{6,2},{7,3},{8,4},{9,5},{10,6},{11,7},{12,8},{13,9},{1... | collective-permute-start | bytes 393224 | tf_op jit(solution)/shard_map/ppermute | solution.py:22
  150.3 24.8 %collective-permute-start.8 = (bf16[16,32,128]{2,1,0:T(8,128)(2,1)S(1)}, bf16[16,32,128]{2,1,0:T(8,128)(2,1)S(1)}, u32[]{:S(2)}, u32[]{:S(2)}) collective-permute-start(bf16[16,32,128]{2,1,0:T(8,128)(2,1)S(1)} %copy-done.1), channel_id=1, source_target_pairs={{0,4},{1,5},{2,6},{3,7},{4,8},{5,9},{6,10},{7,11},{8,12},{9,13},{1... | collective-permute-start | bytes 393224 | tf_op jit(solution)/shard_map/ppermute | solution.py:22
  159.6 19.1 %collective-permute-start.9 = (bf16[16,32,128]{2,1,0:T(8,128)(2,1)S(1)}, bf16[16,32,128]{2,1,0:T(8,128)(2,1)S(1)}, u32[]{:S(2)}, u32[]{:S(2)}) collective-permute-start(bf16[16,32,128]{2,1,0:T(8,128)(2,1)S(1)} %copy-done.1), channel_id=1, source_target_pairs={{0,3},{1,4},{2,5},{3,6},{4,7},{5,8},{6,9},{7,10},{8,11},{9,12},{10... | collective-permute-start | bytes 393224 | tf_op jit(solution)/shard_map/ppermute | solution.py:22
  163.7 17.0 %collective-permute-start.24 = (bf16[32,2048]{1,0:T(8,128)(2,1)S(1)}, bf16[32,2048]{1,0:T(8,128)(2,1)S(1)}, u32[]{:S(2)}, u32[]{:S(2)}) collective-permute-start(bf16[32,2048]{1,0:T(8,128)(2,1)S(1)} %copy-done.11), channel_id=1, source_target_pairs={{0,4},{1,5},{2,6},{3,7},{4,8},{5,9},{6,10},{7,11},{8,12},{9,13},{1... | collective-permute-start | bytes 393224 | tf_op jit(solution)/shard_map/ppermute | solution.py:22
  168.9 13.8 %collective-permute-start.25 = (bf16[32,2048]{1,0:T(8,128)(2,1)S(1)}, bf16[32,2048]{1,0:T(8,128)(2,1)S(1)}, u32[]{:S(2)}, u32[]{:S(2)}) collective-permute-start(bf16[32,2048]{1,0:T(8,128)(2,1)S(1)} %copy-done.11), channel_id=1, source_target_pairs={{0,3},{1,4},{2,5},{3,6},{4,7},{5,8},{6,9},{7,10},{8,11},{9,12},{10... | collective-permute-start | bytes 393224 | tf_op jit(solution)/shard_map/ppermute | solution.py:22
  173.2 17.8 %collective-permute-start.26 = (bf16[32,2048]{1,0:T(8,128)(2,1)S(1)}, bf16[32,2048]{1,0:T(8,128)(2,1)S(1)}, u32[]{:S(2)}, u32[]{:S(2)}) collective-permute-start(bf16[32,2048]{1,0:T(8,128)(2,1)S(1)} %copy-done.11), channel_id=1, source_target_pairs={{0,2},{1,3},{2,4},{3,5},{4,6},{5,7},{6,8},{7,9},{8,10},{9,11},{10,... | collective-permute-start | bytes 393224 | tf_op jit(solution)/shard_map/ppermute | solution.py:22
  175.8 17.2 %collective-permute-start.27 = (bf16[32,2048]{1,0:T(8,128)(2,1)S(1)}, bf16[32,2048]{1,0:T(8,128)(2,1)S(1)}, u32[]{:S(2)}, u32[]{:S(2)}) collective-permute-start(bf16[32,2048]{1,0:T(8,128)(2,1)S(1)} %copy-done.11), channel_id=1, source_target_pairs={{0,1},{1,2},{2,3},{3,4},{4,5},{5,6},{6,7},{7,8},{8,9},{9,10},{10,1... | collective-permute-start | bytes 393224 | tf_op jit(solution)/shard_map/ppermute | solution.py:22
  179.4 17.1 %collective-permute-start.28 = (bf16[32,2048]{1,0:T(8,128)(2,1)S(1)}, bf16[32,2048]{1,0:T(8,128)(2,1)S(1)}, u32[]{:S(2)}, u32[]{:S(2)}) collective-permute-start(bf16[32,2048]{1,0:T(8,128)(2,1)S(1)} %copy-done.11), channel_id=1, source_target_pairs={{1,0},{2,1},{3,2},{4,3},{5,4},{6,5},{7,6},{8,7},{9,8},{10,9},{11,1... | collective-permute-start | bytes 393224 | tf_op jit(solution)/shard_map/ppermute | solution.py:22
  181.3 17.1 %collective-permute-start.29 = (bf16[32,2048]{1,0:T(8,128)(2,1)S(1)}, bf16[32,2048]{1,0:T(8,128)(2,1)S(1)}, u32[]{:S(2)}, u32[]{:S(2)}) collective-permute-start(bf16[32,2048]{1,0:T(8,128)(2,1)S(1)} %copy-done.11), channel_id=1, source_target_pairs={{2,0},{3,1},{4,2},{5,3},{6,4},{7,5},{8,6},{9,7},{10,8},{11,9},{12,... | collective-permute-start | bytes 393224 | tf_op jit(solution)/shard_map/ppermute | solution.py:22
  183.3 26.6 %collective-permute-start.32 = (bf16[8,128,128]{2,1,0:T(8,128)(2,1)}, bf16[8,128,128]{2,1,0:T(8,128)(2,1)S(1)}, u32[]{:S(2)}, u32[]{:S(2)}) collective-permute-start(bf16[8,128,128]{2,1,0:T(8,128)(2,1)} %get-tuple-element.22), channel_id=1, source_target_pairs={{0,4},{1,5},{2,6},{3,7},{4,8},{5,9},{6,10},{7,11},{8,12},{9,13},{1... | collective-permute-start | bytes 786440 | tf_op jit(solution)/shard_map/ppermute | solution.py:22
  191.7 19.6 %collective-permute-start.33 = (bf16[8,128,128]{2,1,0:T(8,128)(2,1)}, bf16[8,128,128]{2,1,0:T(8,128)(2,1)S(1)}, u32[]{:S(2)}, u32[]{:S(2)}) collective-permute-start(bf16[8,128,128]{2,1,0:T(8,128)(2,1)} %get-tuple-element.21), channel_id=1, source_target_pairs={{0,3},{1,4},{2,5},{3,6},{4,7},{5,8},{6,9},{7,10},{8,11},{9,12},{10... | collective-permute-start | bytes 786440 | tf_op jit(solution)/shard_map/ppermute | solution.py:22
  193.6 18.9 %collective-permute-start.34 = (bf16[8,128,128]{2,1,0:T(8,128)(2,1)}, bf16[8,128,128]{2,1,0:T(8,128)(2,1)S(1)}, u32[]{:S(2)}, u32[]{:S(2)}) collective-permute-start(bf16[8,128,128]{2,1,0:T(8,128)(2,1)} %get-tuple-element.20), channel_id=1, source_target_pairs={{0,2},{1,3},{2,4},{3,5},{4,6},{5,7},{6,8},{7,9},{8,10},{9,11},{10,... | collective-permute-start | bytes 786440 | tf_op jit(solution)/shard_map/ppermute | solution.py:22
  197.2 6.3 %collective-permute-start.30 = (bf16[32,2048]{1,0:T(8,128)(2,1)S(1)}, bf16[32,2048]{1,0:T(8,128)(2,1)S(1)}, u32[]{:S(2)}, u32[]{:S(2)}) collective-permute-start(bf16[32,2048]{1,0:T(8,128)(2,1)S(1)} %copy-done.11), channel_id=1, source_target_pairs={{3,0},{4,1},{5,2},{6,3},{7,4},{8,5},{9,6},{10,7},{11,8},{12,9},{13... | collective-permute-start | bytes 393224 | tf_op jit(solution)/shard_map/ppermute | solution.py:22
  199.1 8.9 %collective-permute-start.31 = (bf16[32,2048]{1,0:T(8,128)(2,1)S(1)}, bf16[32,2048]{1,0:T(8,128)(2,1)S(1)}, u32[]{:S(2)}, u32[]{:S(2)}) collective-permute-start(bf16[32,2048]{1,0:T(8,128)(2,1)S(1)} %copy-done.11), channel_id=1, source_target_pairs={{4,0},{5,1},{6,2},{7,3},{8,4},{9,5},{10,6},{11,7},{12,8},{13,9},{1... | collective-permute-start | bytes 393224 | tf_op jit(solution)/shard_map/ppermute | solution.py:22
  204.1 35.0 %collective-permute-start.35 = (bf16[8,128,128]{2,1,0:T(8,128)(2,1)}, bf16[8,128,128]{2,1,0:T(8,128)(2,1)S(1)}, u32[]{:S(2)}, u32[]{:S(2)}) collective-permute-start(bf16[8,128,128]{2,1,0:T(8,128)(2,1)} %get-tuple-element.19), channel_id=1, source_target_pairs={{0,1},{1,2},{2,3},{3,4},{4,5},{5,6},{6,7},{7,8},{8,9},{9,10},{10,1... | collective-permute-start | bytes 786440 | tf_op jit(solution)/shard_map/ppermute | solution.py:22
  208.6 30.4 %collective-permute-start.36 = (bf16[8,128,128]{2,1,0:T(8,128)(2,1)}, bf16[8,128,128]{2,1,0:T(8,128)(2,1)S(1)}, u32[]{:S(2)}, u32[]{:S(2)}) collective-permute-start(bf16[8,128,128]{2,1,0:T(8,128)(2,1)} %get-tuple-element.18), channel_id=1, source_target_pairs={{1,0},{2,1},{3,2},{4,3},{5,4},{6,5},{7,6},{8,7},{9,8},{10,9},{11,1... | collective-permute-start | bytes 786440 | tf_op jit(solution)/shard_map/ppermute | solution.py:22
  209.9 29.1 %collective-permute-start.37 = (bf16[8,128,128]{2,1,0:T(8,128)(2,1)}, bf16[8,128,128]{2,1,0:T(8,128)(2,1)}, u32[]{:S(2)}, u32[]{:S(2)}) collective-permute-start(bf16[8,128,128]{2,1,0:T(8,128)(2,1)} %get-tuple-element.17), channel_id=1, source_target_pairs={{2,0},{3,1},{4,2},{5,3},{6,4},{7,5},{8,6},{9,7},{10,8},{11,9},{12,... | collective-permute-start | bytes 786440 | tf_op jit(solution)/shard_map/ppermute | solution.py:22
  211.2 27.8 %collective-permute-start.38 = (bf16[8,128,128]{2,1,0:T(8,128)(2,1)}, bf16[8,128,128]{2,1,0:T(8,128)(2,1)}, u32[]{:S(2)}, u32[]{:S(2)}) collective-permute-start(bf16[8,128,128]{2,1,0:T(8,128)(2,1)} %get-tuple-element.23), channel_id=1, source_target_pairs={{3,0},{4,1},{5,2},{6,3},{7,4},{8,5},{9,6},{10,7},{11,8},{12,9},{13... | collective-permute-start | bytes 786440 | tf_op jit(solution)/shard_map/ppermute | solution.py:22
  212.6 26.6 %collective-permute-start.39 = (bf16[8,128,128]{2,1,0:T(8,128)(2,1)}, bf16[8,128,128]{2,1,0:T(8,128)(2,1)}, u32[]{:S(2)}, u32[]{:S(2)}) collective-permute-start(bf16[8,128,128]{2,1,0:T(8,128)(2,1)} %get-tuple-element.16), channel_id=1, source_target_pairs={{4,0},{5,1},{6,2},{7,3},{8,4},{9,5},{10,6},{11,7},{12,8},{13,9},{1... | collective-permute-start | bytes 786440 | tf_op jit(solution)/shard_map/ppermute | solution.py:22
  257.8 22.5 %collective-permute-start.40 = (bf16[32,2048]{1,0:T(8,128)(2,1)}, bf16[32,2048]{1,0:T(8,128)(2,1)S(1)}, u32[]{:S(2)}, u32[]{:S(2)}) collective-permute-start(bf16[32,2048]{1,0:T(8,128)(2,1)} %get-tuple-element.7.refs_1_), channel_id=1, source_target_pairs={{0,4},{1,5},{2,6},{3,7},{4,8},{5,9},{6,10},{7,11},{8,12},{9,13},{1... | collective-permute-start | bytes 393224 | tf_op jit(solution)/shard_map/ppermute | solution.py:22
  269.4 12.2 %collective-permute-start.41 = (bf16[32,2048]{1,0:T(8,128)(2,1)}, bf16[32,2048]{1,0:T(8,128)(2,1)S(1)}, u32[]{:S(2)}, u32[]{:S(2)}) collective-permute-start(bf16[32,2048]{1,0:T(8,128)(2,1)} %get-tuple-element.7.refs_1_), channel_id=1, source_target_pairs={{0,3},{1,4},{2,5},{3,6},{4,7},{5,8},{6,9},{7,10},{8,11},{9,12},{10... | collective-permute-start | bytes 393224 | tf_op jit(solution)/shard_map/ppermute | solution.py:22
  272.8 10.2 %collective-permute-start.42 = (bf16[32,2048]{1,0:T(8,128)(2,1)}, bf16[32,2048]{1,0:T(8,128)(2,1)S(1)}, u32[]{:S(2)}, u32[]{:S(2)}) collective-permute-start(bf16[32,2048]{1,0:T(8,128)(2,1)} %get-tuple-element.7.refs_1_), channel_id=1, source_target_pairs={{0,2},{1,3},{2,4},{3,5},{4,6},{5,7},{6,8},{7,9},{8,10},{9,11},{10,... | collective-permute-start | bytes 393224 | tf_op jit(solution)/shard_map/ppermute | solution.py:22
  277.6 51.6 %collective-permute-start.43 = (bf16[32,2048]{1,0:T(8,128)(2,1)}, bf16[32,2048]{1,0:T(8,128)(2,1)S(1)}, u32[]{:S(2)}, u32[]{:S(2)}) collective-permute-start(bf16[32,2048]{1,0:T(8,128)(2,1)} %get-tuple-element.7.refs_1_), channel_id=1, source_target_pairs={{0,1},{1,2},{2,3},{3,4},{4,5},{5,6},{6,7},{7,8},{8,9},{9,10},{10,1... | collective-permute-start | bytes 393224 | tf_op jit(solution)/shard_map/ppermute | solution.py:22
  279.0 50.1 %collective-permute-start.44 = (bf16[32,2048]{1,0:T(8,128)(2,1)}, bf16[32,2048]{1,0:T(8,128)(2,1)S(1)}, u32[]{:S(2)}, u32[]{:S(2)}) collective-permute-start(bf16[32,2048]{1,0:T(8,128)(2,1)} %get-tuple-element.7.refs_1_), channel_id=1, source_target_pairs={{1,0},{2,1},{3,2},{4,3},{5,4},{6,5},{7,6},{8,7},{9,8},{10,9},{11,1... | collective-permute-start | bytes 393224 | tf_op jit(solution)/shard_map/ppermute | solution.py:22
  280.3 48.8 %collective-permute-start.45 = (bf16[32,2048]{1,0:T(8,128)(2,1)}, bf16[32,2048]{1,0:T(8,128)(2,1)S(1)}, u32[]{:S(2)}, u32[]{:S(2)}) collective-permute-start(bf16[32,2048]{1,0:T(8,128)(2,1)} %get-tuple-element.7.refs_1_), channel_id=1, source_target_pairs={{2,0},{3,1},{4,2},{5,3},{6,4},{7,5},{8,6},{9,7},{10,8},{11,9},{12,... | collective-permute-start | bytes 393224 | tf_op jit(solution)/shard_map/ppermute | solution.py:22
  281.6 47.5 %collective-permute-start.46 = (bf16[32,2048]{1,0:T(8,128)(2,1)}, bf16[32,2048]{1,0:T(8,128)(2,1)S(1)}, u32[]{:S(2)}, u32[]{:S(2)}) collective-permute-start(bf16[32,2048]{1,0:T(8,128)(2,1)} %get-tuple-element.7.refs_1_), channel_id=1, source_target_pairs={{3,0},{4,1},{5,2},{6,3},{7,4},{8,5},{9,6},{10,7},{11,8},{12,9},{13... | collective-permute-start | bytes 393224 | tf_op jit(solution)/shard_map/ppermute | solution.py:22
  282.9 46.2 %collective-permute-start.47 = (bf16[32,2048]{1,0:T(8,128)(2,1)}, bf16[32,2048]{1,0:T(8,128)(2,1)S(1)}, u32[]{:S(2)}, u32[]{:S(2)}) collective-permute-start(bf16[32,2048]{1,0:T(8,128)(2,1)} %get-tuple-element.7.refs_1_), channel_id=1, source_target_pairs={{4,0},{5,1},{6,2},{7,3},{8,4},{9,5},{10,6},{11,7},{12,8},{13,9},{1... | collective-permute-start | bytes 393224 | tf_op jit(solution)/shard_map/ppermute | solution.py:22
  (81 other events, 760.9 us)

commit v2 on v1

--- a/solution.py
+++ b/solution.py
@@ -16,12 +16,6 @@
     return lax.dot_general(a, b, dims, preferred_element_type=F32)
 
 
-def shifted(shard, axis, by):
-    size = lax.axis_size(axis)
-    pairs = [(i, i + by) for i in range(size) if 0 <= i + by < size]
-    return lax.ppermute(shard, axis, pairs)
-
-
 def neighbour_offsets(count):
     half = count // 2
     return [step - half if step < half else step - half + 1 for step in range(count)]
@@ -41,6 +35,136 @@
 
 def params():
     return pltpu.CompilerParams(vmem_limit_bytes=40 * 1024 * 1024)
+
+
+def exchange_kernel(owners, offsets, whole, split, filled, *refs):
+    neigh, count = len(offsets), whole + split
+    sources, spread = refs[:count], refs[count]
+    landed, gathered = refs[count + 1 : 2 * count + 1], refs[2 * count + 1]
+    send, recv, spread_send, spread_recv, own = refs[2 * count + 2 :]
+    me = lax.axis_index("leaf")
+    barrier = pltpu.get_barrier_semaphore()
+
+    def greet(i, carry):
+        peer = lax.rem(me + i, owners)
+        pl.semaphore_signal(
+            barrier, inc=1, device_id={"leaf": peer}, device_id_type=pl.DeviceIdType.MESH
+        )
+        return carry
+
+    lax.fori_loop(1, owners, greet, 0)
+
+    def present(k):
+        return (me + offsets[k] >= 0) & (me + offsets[k] < owners)
+
+    if filled is not None:
+        for k in range(neigh):
+
+            @pl.when(jnp.logical_not(present(k)))
+            def _():
+                landed[filled][k] = jnp.full_like(landed[filled].at[k], -1)
+
+    mine = pltpu.make_async_copy(spread_of(spread, me), gathered.at[me], own)
+    mine.start()
+    pl.semaphore_wait(barrier, owners - 1)
+
+    def spread_copy(i):
+        peer = lax.rem(me + i, owners)
+        return pltpu.make_async_remote_copy(
+            src_ref=spread_of(spread, peer),
+            dst_ref=gathered.at[me],
+            send_sem=spread_send.at[i],
+            recv_sem=spread_recv.at[i],
+            device_id={"leaf": peer},
+            device_id_type=pl.DeviceIdType.MESH,
+        )
+
+    def spread_arrival(i):
+        sender = lax.rem(me + owners - i, owners)
+        return pltpu.make_async_remote_copy(
+            src_ref=spread_of(spread, sender),
+            dst_ref=gathered.at[sender],
+            send_sem=spread_send.at[i],
+            recv_sem=spread_recv.at[i],
+            device_id={"leaf": sender},
+            device_id_type=pl.DeviceIdType.MESH,
+        )
+
+    def copy(item, k, slot):
+        source = sources[item] if item < whole else sources[item].at[k]
+        return pltpu.make_async_remote_copy(
+            src_ref=source,
+            dst_ref=landed[item].at[slot],
+            send_sem=send.at[item, k],
+            recv_sem=recv.at[item, slot],
+            device_id={"leaf": me + offsets[k]},
+            device_id_type=pl.DeviceIdType.MESH,
+        )
+
+    for k in range(neigh):
+
+        @pl.when(present(k))
+        def _():
+            for item in range(count):
+                copy(item, k, neigh - 1 - k).start()
+
+    def begin(i, carry):
+        spread_copy(i).start()
+        return carry
+
+    def finish(i, carry):
+        spread_copy(i).wait_send()
+        spread_arrival(i).wait_recv()
+        return carry
+
+    lax.fori_loop(1, owners, begin, 0)
+    mine.wait()
+    lax.fori_loop(1, owners, finish, 0)
+    for k in range(neigh):
+
+        @pl.when(present(k))
+        def _():
+            for item in range(count):
+                copy(item, k, k).wait_send()
+                copy(item, k, k).wait_recv()
+
+
+def spread_of(ref, owner):
+    return ref.at[owner] if len(ref.shape) == 3 else ref
+
+
+def exchange_call(ident, owners, offsets, whole, split, spread, filled=None):
+    neigh = len(offsets)
+    any_space = pl.BlockSpec(memory_space=pl.ANY)
+    specs = [any_space] * (len(whole) + len(split))
+    if filled is not None:
+        specs[filled] = vmem()
+    shapes = [jax.ShapeDtypeStruct((neigh,) + a.shape, a.dtype) for a in whole]
+    shapes += [jax.ShapeDtypeStruct(a.shape, a.dtype) for a in split]
+    shapes += [jax.ShapeDtypeStruct((owners,) + spread.shape[-2:], spread.dtype)]
+
+    def kernel(*refs):
+        exchange_kernel(owners, offsets, len(whole), len(split), filled, *refs)
+
+    items = (len(whole) + len(split), neigh)
+    return pl.pallas_call(
+        kernel,
+        out_shape=tuple(shapes),
+        in_specs=specs + [any_space],
+        out_specs=tuple(specs + [any_space]),
+        scratch_shapes=[
+            pltpu.SemaphoreType.DMA(items),
+            pltpu.SemaphoreType.DMA(items),
+            pltpu.SemaphoreType.DMA((owners,)),
+            pltpu.SemaphoreType.DMA((owners,)),
+            pltpu.SemaphoreType.DMA,
+        ],
+        compiler_params=pltpu.CompilerParams(
+            collective_id=ident, has_side_effects=True, vmem_limit_bytes=40 * 1024 * 1024
+        ),
+        cost_estimate=pl.CostEstimate(flops=0, bytes_accessed=4 * 10**6, transcendentals=0),
+        name="exchange",
+    )(*whole, *split, spread)
 
 
 def start_kernel(x_ref, bases_ref, transfers_ref, v_ref, u_ref):
@@ -138,19 +262,18 @@
 
 
 def far_kernel(neigh, cap, slots_ref, back_ref, mine_ref, far_ref, *refs):
-    peers, got = refs[:neigh], refs[neigh : 2 * neigh]
-    ahead_ref, behind_ref = refs[2 * neigh :]
+    peers, got, ahead_ref, behind_ref = refs
     for k in range(neigh):
         for c in range(cap):
             place = (k * cap + c) * 2
             target = jnp.maximum(slots_ref[place], 0)
             source = jnp.maximum(slots_ref[place + 1], 0)
             lifted = mm(far_ref[k, c], mine_ref[target], TN).astype(BF16)
-            ahead_ref[k, c] = mm(peers[k][source], lifted, TN).astype(BF16)
+            ahead_ref[k, c] = mm(peers[k, source], lifted, TN).astype(BF16)
             target = jnp.maximum(back_ref[place], 0)
             source = jnp.maximum(back_ref[place + 1], 0)
-            lifted = mm(got[k][c], mine_ref[source]).astype(BF16)
-            behind_ref[k, c] = mm(peers[k][target], lifted, TN).astype(BF16)
+            lifted = mm(got[k, c], mine_ref[source]).astype(BF16)
+            behind_ref[k, c] = mm(peers[k, target], lifted, TN).astype(BF16)
 
 
 def far_call(slots, back, bases, blocks, peer_bases, peer_blocks):
@@ -164,29 +287,29 @@
     return pl.pallas_call(
         kernel,
         out_shape=(shape, shape),
-        in_specs=[smem(), smem()] + [vmem()] * (2 + 2 * neigh),
+        in_specs=[smem(), smem()] + [vmem()] * 4,
         out_specs=(vmem(), vmem()),
         compiler_params=params(),
         cost_estimate=pl.CostEstimate(flops=10**8, bytes_accessed=4 * 10**6, transcendentals=0),
         name="far_blocks",
-    )(slots, back, bases, blocks, *peer_bases, *peer_blocks)
+    )(slots, back, bases, blocks, peer_bases, peer_blocks)
 
 
 def join_kernel(
     neigh, near_ref, nback_ref, far_ref, fback_ref, local_ref, v_ref, w_ref, u_ref,
     blocks_ref, ahead_ref, behind_ref, *refs
 ):
-    fields, got = refs[:neigh], refs[neigh : 2 * neigh]
-    out_ref, next_ref, acc_a, acc_b = refs[2 * neigh :]
+    fields, got, out_ref, next_ref, acc_a, acc_b = refs
+    rank = v_ref.shape[0]
     leaves, rows, width = local_ref.shape
     acc_a[:leaves] = local_ref[...]
     acc_b[...] = jnp.zeros_like(acc_b)
     near_cap, far_cap = blocks_ref.shape[1], ahead_ref.shape[1]
 
     def parent(e, total):
-        return total + mm(u_ref[e], w_ref[e])
-
-    total = lax.fori_loop(0, u_ref.shape[0], parent, jnp.zeros(next_ref.shape, F32))
+        return total + mm(u_ref[e][:, :rank], w_ref[e])
+
+    total = lax.fori_loop(0, u_ref.shape[0], parent, jnp.zeros((rows, rank), F32))
     down = total.astype(BF16)
 
     for k in range(neigh):
@@ -194,7 +317,7 @@
         for c in range(near_cap + far_cap):
             if c < near_cap:
                 go, back, place = near_ref, nback_ref, (k * near_cap + c) * 2
-                ahead, behind, dims = blocks_ref[k, c], got[k][c], NT
+                ahead, behind, dims = blocks_ref[k, c], got[k, c], NT
             else:
                 go, back, place = far_ref, fback_ref, (k * far_cap + c - near_cap) * 2
                 ahead, behind, dims = ahead_ref[k, c - near_cap], behind_ref[k, c - near_cap], NN
@@ -204,8 +327,8 @@
                 (
                     jnp.where(target < 0, leaves, target),
                     jnp.where(here < 0, leaves, here),
-                    mm(leaf_cols(fields[k], jnp.maximum(source, 0), width), ahead),
-                    mm(leaf_cols(fields[k], jnp.maximum(there, 0), width), behind, dims),
+                    mm(leaf_cols(fields.at[k], jnp.maximum(source, 0), width), ahead),
+                    mm(leaf_cols(fields.at[k], jnp.maximum(there, 0), width), behind, dims),
                 )
             )
         for target, here, one, two in work:
@@ -214,7 +337,8 @@
     for leaf in range(leaves):
         cols = slice(leaf * width, (leaf + 1) * width)
         out_ref[:, cols] = (acc_a[leaf] + acc_b[leaf] + mm(down, v_ref[:, cols])).astype(BF16)
-    next_ref[...] = mm(out_ref[...], v_ref[...], NT).astype(BF16)
+    next_ref[...] = jnp.zeros_like(next_ref)
+    next_ref[:, :rank] = mm(out_ref[...], v_ref[...], NT).astype(BF16)
 
 
 def join_call(tables, local_sum, v, w, u_all, blocks, far, fields, got):
@@ -228,15 +352,22 @@
         kernel,
         out_shape=(
             jax.ShapeDtypeStruct((rows, leaves * width), BF16),
-            jax.ShapeDtypeStruct((rows, v.shape[0]), BF16),
+            jax.ShapeDtypeStruct((rows, width), BF16),
         ),
-        in_specs=[smem()] * 4 + [vmem()] * (7 + 2 * neigh),
+        in_specs=[smem()] * 4 + [vmem()] * 9,
         out_specs=(vmem(), vmem()),
         scratch_shapes=[pltpu.VMEM((leaves + 1, rows, width), F32)] * 2,
         compiler_params=params(),
         cost_estimate=pl.CostEstimate(flops=10**9, bytes_accessed=8 * 10**6, transcendentals=0),
         name="near_and_join",
-    )(*tables, local_sum, v, w, u_all, blocks, *far, *fields, *got)
+    )(*tables, local_sum, v, w, u_all, blocks, *far, fields, got)
+
+
+def exchange_first(owners, offsets, flat, rhs, bases, near, far, spread):
+    fields, got_bases, flat_got, got_near, got_far, u_all = exchange_call(
+        0, owners, offsets, [rhs, bases], [flat, near, far], spread, filled=2
+    )
+    return flat_got, fields, got_bases, got_near, got_far, u_all
 
 
 def body(
@@ -257,43 +388,45 @@
     near, far = near_blocks[0], far_blocks[0]
     near_cap, far_cap = near.shape[1], far.shape[1]
 
-    def send(pick):
-        return [shifted(pick(neigh - 1 - k), "leaf", -offsets[k]) for k in range(neigh)]
-
-    fields = send(lambda k: rhs)
+    owners = lax.axis_size("leaf")
+    lanes = bases.shape[2]
     slots = jnp.concatenate([near_slots[0], far_slots[0]], axis=1)
-    back = jnp.stack(send(lambda k: slots[k]))
-    got_bases = send(lambda k: bases)
-    got_far = send(lambda k: far[k])
-    got_near = send(lambda k: near[k])
+    flat = slots.reshape(neigh, 1, -1)
+    flat = jnp.pad(flat, ((0, 0), (0, 7), (0, lanes - flat.shape[2])))
+
+    v, u = start_call(rhs, bases, transfers)
+
+    ids = jnp.arange(owners, dtype=jnp.int32)
+    live = (parent_pairs[0][:, None] == ids[None, :]).astype(F32)[:, :, None, None]
+    parents = parent_blocks[0].astype(F32)
+    returned = jnp.sum(live * parents[:, None], axis=0).astype(BF16)
+    rank = returned.shape[1]
+    spread = jnp.concatenate(
+        [
+            jnp.broadcast_to(u[None], (owners,) + u.shape),
+            returned,
+            jnp.zeros((owners, rank, lanes - 2 * rank), BF16),
+        ],
+        axis=2,
+    )
+    flat_got, fields, got_bases, got_near, got_far, u_all = exchange_first(
+        owners, offsets, flat, rhs, bases, near, far, spread
+    )
+    back = flat_got[:, 0, : 2 * (near_cap + far_cap)].reshape(neigh, near_cap + far_cap, 2)
     tables = [
         near_slots.reshape(-1),
         back[:, :near_cap].reshape(-1),
         far_slots.reshape(-1),
         back[:, near_cap:].reshape(-1),
     ]
-
-    v, u = start_call(rhs, bases, transfers)
-
-    owners = lax.axis_size("leaf")
-    me = lax.axis_index("leaf")
-    all_blocks = lax.all_gather(parent_blocks[0], "leaf", axis=0)
-    all_pairs = lax.all_gather(parent_pairs[0], "leaf", axis=0)
-    ids = jnp.arange(owners, dtype=jnp.int32)
-    mine = (parent_pairs[0][:, None] == ids[None, :]).astype(F32)
-    theirs = (all_pairs == me).astype(F32)
-    w = jnp.sum(
-        mine[:, :, None, None] * parent_blocks[0].astype(F32).transpose(0, 2, 1)[:, None], axis=0
-    ) + jnp.sum(theirs[:, :, None, None] * all_blocks.astype(F32), axis=1)
-    w = w.astype(BF16)
-
-    u_all = lax.all_gather(u, "leaf", axis=0)
+    w = jnp.sum(live * parents.transpose(0, 2, 1)[:, None], axis=0)
+    w = (w + u_all[:, :, rank : 2 * rank].astype(F32)).astype(BF16)
+
     local_sum = local_call(rhs, local_pairs[0], local_blocks[0])
     effective = far_call(tables[2], tables[3], bases, far, got_bases, got_far)
     first, u = join_call(tables, local_sum, v, w, u_all, near, effective, fields, got_near)
 
-    fields = send(lambda k: first)
-    u_all = lax.all_gather(u, "leaf", axis=0)
+    fields, u_all = exchange_call(1, owners, offsets, [first], [], u)
     local_sum = local_call(first, local_pairs[0], local_blocks[0])
     second, _ = join_call(tables, local_sum, v, w, u_all, near, effective, fields, got_near)
     return (first, second)

time: 338 us -> 147 us (0.43)
  starting transfers between devices: 125 us -> 0 us
  blocking collectives: 87.3 us -> 0 us
  Pallas kernels: 41 us -> 114 us
  local copies, waits for them, and re-layouts: 71.3 us -> 29.1 us
  waiting for transfers between devices: 7.3 us -> 0 us
    ppermute x48 -> x0, starting transfers between devices: 125 us -> none  [shifted(): return lax.ppermute(shard, axis, pairs)]
    all_gather x4 -> x0, blocking collectives: 87.3 us -> none  [the longest x2 48 us: body(): u_all = lax.all_gather(u, 'leaf', axis=0)]
    pallas_call x0 -> x2, Pallas kernels: none -> 74 us  [exchange_call(): pl.pallas_call(kernel, out_shape=tuple(shapes), in_specs=specs + [any_spa...]
    unnamed x173 -> x56, local copies, waits for them, and re-layouts: 58.3 us -> 26.2 us
    ppermute x48 -> x0, waiting for transfers between devices: 7.3 us -> none  [shifted(): return lax.ppermute(shard, axis, pairs)]
    squeeze x2 -> x0, local copies, waits for them, and re-layouts: 4.34 us -> none  [the longest x1 2.89 us: body(): got_near = send(lambda k: near[k])]
  transfers between devices with their start and end apart: 48 -> 0, of which waited for: 6 -> 0; matrix products, arithmetic and copies ran while one was open for 6% -> 0% of each run, Pallas kernels for 9% -> 0%
where the time goes in v2:
time: 147 us; the launch traced here: 146 us
  Pallas kernels  114 us (78%)
  local copies, waits for them, and re-layouts  29.1 us (20%)
  other arithmetic  2.06 us (1%)
    pallas_call x2, Pallas kernels, exchange_call(): pl.pallas_call(kernel, out_shape=tuple(shapes), in_specs=specs + [any_spa...  74 us
    unnamed x56, local copies, waits for them, and re-layouts  26.2 us
    pallas_call x2, Pallas kernels, local_call(): pl.pallas_call(kernel, grid=(steps,), out_shape=jax.ShapeDtypeStruct(shap...  25.6 us
    pallas_call x2, Pallas kernels, join_call(): pl.pallas_call(kernel, out_shape=(jax.ShapeDtypeStruct((rows, leaves * wi...  11.1 us

profile of v2, /device:TPU:0, one launch (start us, length us, event | category | flops | bytes accessed | tf_op | source)
XLA Modules:
  0.0 145.9 jit_solution(15916367019536914900)
XLA Ops:
  0.6 0.8 bitcast_convert_fusion
  1.4 0.1 copy.40
  1.5 0.7 fusion.1
  2.2 0.3 multiply_reduce_fusion
  2.5 0.9 copy-done.5
  3.4 0.9 copy-done.12
  4.3 0.9 copy-done.17
  5.2 0.3 parent_basis.1
  5.7 0.1 maximum_maximum_fusion.refs_5_
  5.8 0.7 copy.42
  6.5 0.8 copy.32
  7.2 0.1 pad_add_fusion
  7.3 0.1 copy.33
  7.4 0.1 copy.34
  7.5 1.6 %copy-done = bf16[1,8,8,128,128]{4,3,2,1,0:T(8,128)(2,1)S(1)} copy-done((bf16[1,8,8,128,128]{4,3,2,1,0:T(8,128)(2,1)S(1)}, bf16[1,8,8,128,128]{4,3,2,1,0:T(8,128)(2,1)}, u32[]{:S(2)}) %copy-start) | copy-done | bytes 2097176
  9.1 0.9 copy-done.6
  10.0 0.9 copy-done.10
  10.9 0.9 copy-done.13
  11.8 55.8 %exchange.2 = (bf16[8,32,2048]{2,1,0:T(8,128)(2,1)S(1)}, bf16[8,16,32,128]{3,2,1,0:T(8,128)(2,1)S(1)}, s32[8,8,128]{2,1,0:T(8,128)S(1)}, bf16[8,8,128,128]{3,2,1...) custom-call(bf16[32,2048]{1,0:T(8,128)(2,1)S(1)} %copy-done.13, ...), custom_call_target="tpu_custom_call" | custom-call | bytes 4000000 | tf_op jit(solution)/shard_map/exchange/pallas_call | solution.py:150
  67.6 1.3 copy-done.2
  69.0 1.0 copy-done.8
  70.0 0.1 copy.35
  70.1 0.1 copy.38
  70.2 0.1 reshape.57.refs_1_.refs_3_
  70.3 0.1 copy.37
  70.4 0.1 reshape.56.refs_0_.refs_2_
  70.5 2.9 %far_blocks.1 = (bf16[8,2,128,128]{3,2,1,0:T(8,128)(2,1)S(1)}, bf16[8,2,128,128]{3,2,1,0:T(8,128)(2,1)S(1)}) custom-call(s32[32]{0:T(128)S(1)} %reshape.56.refs_0_.refs_2_, s32[32]{0:T(128)S(1)} %reshape.57.refs_1_.refs_3_, bf16[16,32,128]{2,1,0:T(8,128)(2,1)S(1)} %copy-done.7, bf16[8,2,32,32]{3,2,1,0:T(8,128)(2,1)S(1)} %bitcast.25, ...), custom_call_target="tpu_custom_call" | custom-call | flops 100000000 | bytes 4000000 | tf_op jit(solution)/shard_map/far_blocks/pallas_call | solution.py:287
  73.4 0.1 add_convert_fusion.refs_6_
  73.5 0.1 copy.36
  73.7 0.1 reshape.55.refs_1_
  73.8 0.1 copy.39
  74.0 0.1 reshape_squeeze.8.refs_0_
  74.1 0.9 copy-done.14
  75.0 3.7 %copy-done.22 = bf16[1,288,128,128]{3,2,1,0:T(8,128)(2,1)S(1)} copy-done((bf16[1,288,128,128]{3,2,1,0:T(8,128)(2,1)S(1)}, bf16[1,288,128,128]{3,2,1,0:T(8,128)(2,1)}, u32[]{:S(2)}) %copy-start.22) | copy-done | bytes 9437208
  78.7 12.8 %local_blocks.2.refs_4_ = f32[16,32,128]{2,1,0:T(8,128)S(1)} custom-call(s32[576]{0:T(1024)S(1)} %reshape_squeeze.8.refs_0_, bf16[32,2048]{1,0:T(8,128)(2,1)S(1)} %copy-done.14, bf16[288,128,128]{2,1,0:T(8,128)(2,1)S(1)} %bitcast.26), custom_call_target="tpu_custom_call" | custom-call | flops 9663676416 | bytes 9437184 | tf_op jit(solution)/shard_map/local_blocks/pallas_call | solution.py:243
  91.5 0.7 copy-done.15
  92.2 1.4 copy.30
  93.7 0.9 reshape.53.refs_0_
  94.6 1.6 %copy-done.3 = bf16[8,8,128,128]{3,2,1,0:T(8,128)(2,1)S(1)} copy-done((bf16[8,8,128,128]{3,2,1,0:T(8,128)(2,1)S(1)}, bf16[8,8,128,128]{3,2,1,0:T(8,128)(2,1)}, u32[]{:S(2)}) %copy-start.3) | copy-done | bytes 2097176
  96.2 1.2 copy-done.9
  97.4 0.9 copy-done.16
  98.3 5.5 %near_and_join.2 = (bf16[32,2048]{1,0:T(8,128)(2,1)}, bf16[32,128]{1,0:T(8,128)(2,1)S(1)}) custom-call(s32[128]{0:T(128)S(1)} %reshape.53.refs_0_, s32[128]{0:T(128)S(1)} %reshape.55.refs_1_, s32[32]{0:T(128)S(1)} %reshape.56.refs_0_.refs_2_, s32[32]{0:T(128)S(1)} %reshape.57.refs_1_.refs_3_, f32[16,32,128]{2,1,0:T(8,128)S(1)} %copy-done.16, ...), custom_call_target="tpu_custom_call" | custom-call | flops 1000000000 | bytes 8000000 | tf_op jit(solution)/shard_map/near_and_join/pallas_call | solution.py:351
  103.8 0.9 copy-done.18
  104.7 18.2 %exchange.3 = (bf16[8,32,2048]{2,1,0:T(8,128)(2,1)S(1)}, bf16[16,32,128]{2,1,0:T(8,128)(2,1)S(1)}) custom-call(bf16[32,2048]{1,0:T(8,128)(2,1)S(1)} %copy-done.18, bf16[32,128]{1,0:T(8,128)(2,1)S(1)} %get-tuple-element.28.refs_1_), custom_call_target="tpu_custom_call" | custom-call | bytes 4000000 | tf_op jit(solution)/shard_map/exchange/pallas_call | solution.py:150
  122.9 0.9 copy-done.19
  123.8 3.7 %copy-done.23 = bf16[1,288,128,128]{3,2,1,0:T(8,128)(2,1)S(1)} copy-done((bf16[1,288,128,128]{3,2,1,0:T(8,128)(2,1)S(1)}, bf16[1,288,128,128]{3,2,1,0:T(8,128)(2,1)}, u32[]{:S(2)}) %copy-start.23) | copy-done | bytes 9437208
  127.5 12.8 %local_blocks.3.refs_4_ = f32[16,32,128]{2,1,0:T(8,128)S(1)} custom-call(s32[576]{0:T(1024)S(1)} %copy-done.21, bf16[32,2048]{1,0:T(8,128)(2,1)S(1)} %copy-done.19, bf16[288,128,128]{2,1,0:T(8,128)(2,1)S(1)} %bitcast.27), custom_call_target="tpu_custom_call" | custom-call | flops 9663676416 | bytes 9437184 | tf_op jit(solution)/shard_map/local_blocks/pallas_call | solution.py:243
  140.3 5.6 %near_and_join.3 = (bf16[32,2048]{1,0:T(8,128)(2,1)}, bf16[32,128]{1,0:T(8,128)(2,1)}) custom-call(s32[128]{0:T(128)S(1)} %reshape.53.refs_0_, s32[128]{0:T(128)S(1)} %reshape.55.refs_1_, s32[32]{0:T(128)S(1)} %reshape.56.refs_0_.refs_2_, s32[32]{0:T(128)S(1)} %reshape.57.refs_1_.refs_3_, f32[16,32,128]{2,1,0:T(8,128)S(1)} %local_blocks.3.refs_4_, ...), custom_call_target="tpu_custom_call" | custom-call | flops 1000000000 | bytes 8000000 | tf_op jit(solution)/shard_map/near_and_join/pallas_call | solution.py:351
  (43 shorter events, 0.2 us)
Async XLA Ops:
  2.2 68.1 %copy-start.24 = (s32[1,8,2,2]{1,3,2,0:T(2,128)S(1)}, s32[1,8,2,2]{1,3,2,0:T(2,128)}, u32[]{:S(2)}) copy-start(s32[1,8,2,2]{1,3,2,0:T(2,128)} %param.18) | copy-start | bytes 388
  2.2 68.2 %copy-start.7 = (bf16[16,32,128]{2,1,0:T(8,128)(2,1)S(1)}, bf16[16,32,128]{2,1,0:T(8,128)(2,1)}, u32[]{:S(2)}) copy-start(bf16[16,32,128]{2,1,0:T(8,128)(2,1)} %refs_2_.1) | copy-start | bytes 393220
  2.2 68.3 %copy-start.11 = (bf16[1,8,2,32,32]{4,3,2,1,0:T(8,128)(2,1)S(1)}, bf16[1,8,2,32,32]{4,3,2,1,0:T(8,128)(2,1)}, u32[]{:S(2)}) copy-start(bf16[1,8,2,32,32]{4,3,2,1,0:T(8,128)(2,1)} %param.19) | copy-start | bytes 98308
  2.5 0.9 copy-start.5
  3.4 0.9 copy-start.12
  4.3 0.9 copy-start.17
  7.5 1.6 %copy-start = (bf16[1,8,8,128,128]{4,3,2,1,0:T(8,128)(2,1)S(1)}, bf16[1,8,8,128,128]{4,3,2,1,0:T(8,128)(2,1)}, u32[]{:S(2)}) copy-start(bf16[1,8,8,128,128]{4,3,2,1,0:T(8,128)(2,1)} %param.15) | copy-start | bytes 6291460
  9.1 0.9 copy-start.6
  10.0 0.9 copy-start.10
  10.9 0.9 copy-start.13
  11.8 62.0 %copy-start.25 = (s32[1,288,2]{1,2,0:T(2,128)S(1)}, s32[1,288,2]{1,2,0:T(2,128)}, u32[]{:S(2)}) copy-start(s32[1,288,2]{1,2,0:T(2,128)} %param.16) | copy-start | bytes 6916
  67.6 1.3 copy-start.2
  69.0 1.0 copy-start.8
  74.1 17.4 %copy-start.20 = (s32[576]{0:T(1024)}, s32[576]{0:T(1024)S(1)}, u32[]{:S(2)}) copy-start(s32[576]{0:T(1024)S(1)} %reshape_squeeze.8.refs_0_) | copy-start | bytes 6916
  74.1 0.9 copy-start.14
  75.0 3.7 %copy-start.22 = (bf16[1,288,128,128]{3,2,1,0:T(8,128)(2,1)S(1)}, bf16[1,288,128,128]{3,2,1,0:T(8,128)(2,1)}, u32[]{:S(2)}) copy-start(bf16[1,288,128,128]{3,2,1,0:T(8,128)(2,1)} %param.17) | copy-start | bytes 28311556
  78.7 15.8 %copy-start.1 = (bf16[1,8,8,128,128]{4,3,2,1,0:T(8,128)(2,1)S(1)}, bf16[1,8,8,128,128]{4,3,2,1,0:T(8,128)(2,1)}, u32[]{:S(2)}) copy-start(bf16[1,8,8,128,128]{4,3,2,1,0:T(8,128)(2,1)} %param.15) | copy-start | bytes 6291460
  91.5 0.7 copy-start.15
  94.6 1.6 %copy-start.3 = (bf16[8,8,128,128]{3,2,1,0:T(8,128)(2,1)S(1)}, bf16[8,8,128,128]{3,2,1,0:T(8,128)(2,1)}, u32[]{:S(2)}) copy-start(bf16[8,8,128,128]{3,2,1,0:T(8,128)(2,1)} %copy-done.2) | copy-start | bytes 6291460
  96.1 1.2 copy-start.9
  97.4 0.9 copy-start.16
  98.3 24.6 %copy-start.21 = (s32[576]{0:T(1024)S(1)}, s32[576]{0:T(1024)}, u32[]{:S(2)}) copy-start(s32[576]{0:T(1024)} %copy-done.20) | copy-start | bytes 6916
  103.8 0.9 copy-start.18
  122.9 0.9 copy-start.19
  123.8 3.7 %copy-start.23 = (bf16[1,288,128,128]{3,2,1,0:T(8,128)(2,1)S(1)}, bf16[1,288,128,128]{3,2,1,0:T(8,128)(2,1)}, u32[]{:S(2)}) copy-start(bf16[1,288,128,128]{3,2,1,0:T(8,128)(2,1)} %param.17) | copy-start | bytes 28311556
  127.5 12.8 %copy-start.4 = (bf16[8,8,128,128]{3,2,1,0:T(8,128)(2,1)S(1)}, bf16[8,8,128,128]{3,2,1,0:T(8,128)(2,1)}, u32[]{:S(2)}) copy-start(bf16[8,8,128,128]{3,2,1,0:T(8,128)(2,1)} %copy-done.2) | copy-start | bytes 6291460

commit v3 on v2

--- a/solution.py
+++ b/solution.py
@@ -34,14 +34,14 @@
 
 
 def params():
-    return pltpu.CompilerParams(vmem_limit_bytes=40 * 1024 * 1024)
+    return pltpu.CompilerParams(vmem_limit_bytes=60 * 1024 * 1024)
 
 
 def exchange_kernel(owners, offsets, whole, split, filled, *refs):
     neigh, count = len(offsets), whole + split
     sources, spread = refs[:count], refs[count]
     landed, gathered = refs[count + 1 : 2 * count + 1], refs[2 * count + 1]
-    send, recv, spread_send, spread_recv, own = refs[2 * count + 2 :]
+    send, recv, spread_send, spread_recv, own, onward = refs[2 * count + 2 :]
     me = lax.axis_index("leaf")
     barrier = pltpu.get_barrier_semaphore()
 
@@ -101,11 +101,45 @@
             device_id_type=pl.DeviceIdType.MESH,
         )
 
+    parity = lax.rem(me, 2)
+
+    def direct(k):
+        step = offsets[k]
+        if step % 2 == 0:
+            return present(k)
+        relayed = [step - 1 in offsets, step + 1 in offsets]
+        return present(k) & ((parity == 0) & (not relayed[0]) | (parity == 1) & (not relayed[1]))
+
+    def relay(item, k, side):
+        slot = offsets.index(offsets[k] + (1 if side else -1))
+        return pltpu.make_async_remote_copy(
+            src_ref=landed[item].at[k],
+            dst_ref=landed[item].at[slot],
+            send_sem=onward.at[item, k],
+            recv_sem=recv.at[item, slot],
+            device_id={"leaf": me + (-1 if side else 1)},
+            device_id_type=pl.DeviceIdType.MESH,
+        )
+
+    relays = [
+        (k, side)
+        for k in range(neigh)
+        for side in (0, 1)
+        if offsets[k] % 2 == 0 and offsets[k] + (1 if side else -1) in offsets
+    ]
+
+    for k in range(neigh):
+
+        @pl.when(direct(k))
+        def _():
+            for item in range(whole):
+                copy(item, k, neigh - 1 - k).start()
+
     for k in range(neigh):
 
         @pl.when(present(k))
         def _():
-            for item in range(count):
+            for item in range(whole, count):
                 copy(item, k, neigh - 1 - k).start()
 
     def begin(i, carry):
@@ -121,12 +155,41 @@
     mine.wait()
     lax.fori_loop(1, owners, finish, 0)
     for k in range(neigh):
+        if offsets[k] % 2 == 0:
+
+            @pl.when(present(k))
+            def _():
+                for item in range(whole):
+                    copy(item, k, k).wait_recv()
+
+            for place, side in relays:
+                if place == k:
+
+                    @pl.when(present(k) & (parity == side))
+                    def _():
+                        for item in range(whole):
+                            relay(item, k, side).start()
+
+    for k in range(neigh):
+
+        @pl.when(direct(k))
+        def _():
+            for item in range(whole):
+                copy(item, k, k).wait_send()
 
         @pl.when(present(k))
         def _():
-            for item in range(count):
+            for item in range(whole if offsets[k] % 2 == 0 else 0, count):
+                copy(item, k, k).wait_recv()
+            for item in range(whole, count):
                 copy(item, k, k).wait_send()
-                copy(item, k, k).wait_recv()
+
+    for k, side in relays:
+
+        @pl.when(present(k) & (parity == side))
+        def _():
+            for item in range(whole):
+                relay(item, k, side).wait_send()
 
 
 def spread_of(ref, owner):
@@ -158,6 +221,7 @@
             pltpu.SemaphoreType.DMA((owners,)),
             pltpu.SemaphoreType.DMA((owners,)),
             pltpu.SemaphoreType.DMA,
+            pltpu.SemaphoreType.DMA(items),
         ],
         compiler_params=pltpu.CompilerParams(
             collective_id=ident, has_side_effects=True, vmem_limit_bytes=40 * 1024 * 1024

time: 147 us -> 135 us (0.918)
  local copies, waits for them, and re-layouts: 29.1 us -> 18 us
    unnamed x56 -> x36, local copies, waits for them, and re-layouts: 26.2 us -> 12.5 us
    pallas_call x2, Pallas kernels: 74 us -> 61.7 us  [exchange_call(): pl.pallas_call(kernel, out_shape=tuple(shapes), in_specs=specs + [any_spa...]
    pallas_call x2, Pallas kernels: 11.1 us -> 16.3 us  [join_call(): pl.pallas_call(kernel, out_shape=(jax.ShapeDtypeStruct((rows, leaves * wi...]
    pallas_call x2, Pallas kernels: 25.6 us -> 28.7 us  [local_call(): pl.pallas_call(kernel, grid=(steps,), out_shape=jax.ShapeDtypeStruct(shap...]
    pallas_call x1, Pallas kernels: 2.92 us -> 4.66 us  [far_call(): pl.pallas_call(kernel, out_shape=(shape, shape), in_specs=[smem(), smem()...]
    pallas_call x1, Pallas kernels: 0.3 us -> 1.95 us  [start_call(): pl.pallas_call(start_kernel, out_shape=(jax.ShapeDtypeStruct((rank, x.sha...]
where the time goes in v3:
time: 135 us
  Pallas kernels  113 us (84%)
  local copies, waits for them, and re-layouts  18 us (13%)
  other arithmetic  2.72 us (2%)
    pallas_call x2, Pallas kernels, exchange_call(): pl.pallas_call(kernel, out_shape=tuple(shapes), in_specs=specs + [any_spa...  61.7 us
    pallas_call x2, Pallas kernels, local_call(): pl.pallas_call(kernel, grid=(steps,), out_shape=jax.ShapeDtypeStruct(shap...  28.7 us
    pallas_call x2, Pallas kernels, join_call(): pl.pallas_call(kernel, out_shape=(jax.ShapeDtypeStruct((rows, leaves * wi...  16.3 us
    unnamed x36, local copies, waits for them, and re-layouts  12.5 us
    pallas_call x1, Pallas kernels, far_call(): pl.pallas_call(kernel, out_shape=(shape, shape), in_specs=[smem(), smem()...  4.66 us

profile of v3, /device:TPU:0, one launch (start us, length us, event | category | flops | bytes accessed | tf_op | source)
XLA Modules:
  0.0 134.8 jit_solution(1038097212844899062)
XLA Ops:
  0.6 0.8 bitcast_convert_fusion
  1.4 0.1 copy.40
  1.5 0.7 fusion.1
  2.2 0.3 multiply_reduce_fusion
  2.5 2.0 %parent_basis.1 = (bf16[32,2048]{1,0:T(8,128)(2,1)}, bf16[32,32]{1,0:T(8,128)(2,1)}) custom-call(bf16[32,2048]{1,0:T(8,128)(2,1)} %refs_1_.3, bf16[16,32,128]{2,1,0:T(8,128)(2,1)} %refs_2_.1, bf16[16,32,32]{2,1,0:T(8,128)(2,1)} %transfers_ref.1), custom_call_target="tpu_custom_call" | custom-call | flops 10000000 | bytes 1000000 | tf_op jit(solution)/shard_map/parent_basis/pallas_call | solution.py:245
  4.4 0.7 broadcast_in_dim.4
  5.2 0.1 pad.7.clone
  5.3 0.1 maximum_maximum_fusion.refs_5_
  5.4 0.7 copy.42
  6.1 0.8 copy.32
  6.8 0.1 pad_add_fusion
  6.9 0.1 copy.33
  7.0 0.1 copy.34
  7.1 1.6 %copy-done = bf16[1,8,8,128,128]{4,3,2,1,0:T(8,128)(2,1)S(1)} copy-done((bf16[1,8,8,128,128]{4,3,2,1,0:T(8,128)(2,1)S(1)}, bf16[1,8,8,128,128]{4,3,2,1,0:T(8,128)(2,1)}, u32[]{:S(2)}) %copy-start) | copy-done | bytes 2097176
  8.7 0.9 copy-done.2
  9.6 0.9 copy-done.7
  10.5 0.9 copy-done.8
  11.4 46.4 %exchange.2 = (bf16[8,32,2048]{2,1,0:T(8,128)(2,1)S(1)}, bf16[8,16,32,128]{3,2,1,0:T(8,128)(2,1)S(1)}, s32[8,8,128]{2,1,0:T(8,128)S(1)}, bf16[8,8,128,128]{3,2,1...) custom-call(bf16[32,2048]{1,0:T(8,128)(2,1)S(1)} %copy-done.8, ...), custom_call_target="tpu_custom_call" | custom-call | bytes 4000000 | tf_op jit(solution)/shard_map/exchange/pallas_call | solution.py:213
  57.8 0.0 copy-start.1
  57.9 1.3 copy-done.1
  59.2 1.0 copy-done.3
  60.2 1.0 copy-done.5
  61.2 0.7 copy-done.9
  61.8 0.1 copy.35
  61.9 0.1 copy.38
  62.0 0.6 reshape.57.refs_1_.refs_3_
  62.6 0.0 copy-done.14
  62.6 0.1 copy.37
  62.7 0.6 reshape.56.refs_0_.refs_2_
  63.4 4.7 %far_blocks.1 = (bf16[8,2,128,128]{3,2,1,0:T(8,128)(2,1)}, bf16[8,2,128,128]{3,2,1,0:T(8,128)(2,1)}) custom-call(s32[32]{0:T(128)} %reshape.56.refs_0_.refs_2_, s32[32]{0:T(128)} %reshape.57.refs_1_.refs_3_, bf16[16,32,128]{2,1,0:T(8,128)(2,1)} %refs_2_.1, bf16[8,2,32,32]{3,2,1,0:T(8,128)(2,1)} %bitcast.24, bf16[8,16,32,128]{3,2,1,0:T(8,128)(2,1)} %copy-done.5, ...), custom_call_target="tpu_custom_call" | custom-call | flops 100000000 | bytes 4000000 | tf_op jit(solution)/shard_map/far_blocks/pallas_call | solution.py:351
  68.0 0.8 add_convert_fusion.refs_6_
  68.8 0.1 copy.36
  68.9 0.7 reshape.55.refs_1_
  69.6 0.0 copy-done.15
  69.6 0.1 copy.39
  69.7 0.7 reshape_squeeze.8.refs_0_
  70.4 14.4 %local_blocks.2.refs_4_ = f32[16,32,128]{2,1,0:T(8,128)} custom-call(s32[576]{0:T(1024)} %reshape_squeeze.8.refs_0_, bf16[32,2048]{1,0:T(8,128)(2,1)} %refs_1_.3, bf16[288,128,128]{2,1,0:T(8,128)(2,1)} %bitcast.29), custom_call_target="tpu_custom_call" | custom-call | flops 9663676416 | bytes 9437184 | tf_op jit(solution)/shard_map/local_blocks/pallas_call | solution.py:307
  84.8 0.0 copy-done.6
  84.8 0.1 copy.30
  84.9 0.7 reshape.53.refs_0_
  85.6 8.1 %near_and_join.2 = (bf16[32,2048]{1,0:T(8,128)(2,1)}, bf16[32,128]{1,0:T(8,128)(2,1)}) custom-call(s32[128]{0:T(128)} %reshape.53.refs_0_, s32[128]{0:T(128)} %reshape.55.refs_1_, s32[32]{0:T(128)} %reshape.56.refs_0_.refs_2_, s32[32]{0:T(128)} %reshape.57.refs_1_.refs_3_, f32[16,32,128]{2,1,0:T(8,128)} %local_blocks.2.refs_4_, ...), custom_call_target="tpu_custom_call" | custom-call | flops 1000000000 | bytes 8000000 | tf_op jit(solution)/shard_map/near_and_join/pallas_call | solution.py:415
  93.8 0.9 copy-done.11
  94.7 0.7 copy-done.12
  95.4 15.3 %exchange.3 = (bf16[8,32,2048]{2,1,0:T(8,128)(2,1)S(1)}, bf16[16,32,128]{2,1,0:T(8,128)(2,1)S(1)}) custom-call(bf16[32,2048]{1,0:T(8,128)(2,1)S(1)} %copy-done.11, bf16[32,128]{1,0:T(8,128)(2,1)S(1)} %copy-done.12), custom_call_target="tpu_custom_call" | custom-call | bytes 4000000 | tf_op jit(solution)/shard_map/exchange/pallas_call | solution.py:213
  110.7 1.0 copy-done.4
  111.7 0.7 copy-done.10
  112.3 14.3 %local_blocks.3.refs_4_ = f32[16,32,128]{2,1,0:T(8,128)} custom-call(s32[576]{0:T(1024)} %reshape_squeeze.8.refs_0_, bf16[32,2048]{1,0:T(8,128)(2,1)} %get-tuple-element.15.refs_1_.refs_0_, bf16[288,128,128]{2,1,0:T(8,128)(2,1)} %bitcast.30), custom_call_target="tpu_custom_call" | custom-call | flops 9663676416 | bytes 9437184 | tf_op jit(solution)/shard_map/local_blocks/pallas_call | solution.py:307
  126.7 8.1 %near_and_join.3 = (bf16[32,2048]{1,0:T(8,128)(2,1)}, bf16[32,128]{1,0:T(8,128)(2,1)}) custom-call(s32[128]{0:T(128)} %reshape.53.refs_0_, s32[128]{0:T(128)} %reshape.55.refs_1_, s32[32]{0:T(128)} %reshape.56.refs_0_.refs_2_, s32[32]{0:T(128)} %reshape.57.refs_1_.refs_3_, f32[16,32,128]{2,1,0:T(8,128)} %local_blocks.3.refs_4_, ...), custom_call_target="tpu_custom_call" | custom-call | flops 1000000000 | bytes 8000000 | tf_op jit(solution)/shard_map/near_and_join/pallas_call | solution.py:415
  (23 shorter events, 0.1 us)
Async XLA Ops:
  2.2 60.4 %copy-start.14 = (s32[1,8,2,2]{1,3,2,0:T(2,128)S(1)}, s32[1,8,2,2]{1,3,2,0:T(2,128)}, u32[]{:S(2)}) copy-start(s32[1,8,2,2]{1,3,2,0:T(2,128)} %param.18) | copy-start | bytes 388
  7.1 1.6 %copy-start = (bf16[1,8,8,128,128]{4,3,2,1,0:T(8,128)(2,1)S(1)}, bf16[1,8,8,128,128]{4,3,2,1,0:T(8,128)(2,1)}, u32[]{:S(2)}) copy-start(bf16[1,8,8,128,128]{4,3,2,1,0:T(8,128)(2,1)} %param.15) | copy-start | bytes 6291460
  8.7 0.9 copy-start.2
  9.6 0.9 copy-start.7
  10.5 0.9 copy-start.8
  11.4 58.2 %copy-start.15 = (s32[1,288,2]{1,2,0:T(2,128)S(1)}, s32[1,288,2]{1,2,0:T(2,128)}, u32[]{:S(2)}) copy-start(s32[1,288,2]{1,2,0:T(2,128)} %param.16) | copy-start | bytes 6916
  57.8 1.3 copy-start.1
  59.2 1.0 copy-start.3
  60.2 1.0 copy-start.5
  61.2 0.7 copy-start.9
  61.8 23.0 %copy-start.6 = (bf16[16,32,128]{2,1,0:T(8,128)(2,1)}, bf16[16,32,128]{2,1,0:T(8,128)(2,1)S(1)}, u32[]{:S(2)}) copy-start(bf16[16,32,128]{2,1,0:T(8,128)(2,1)S(1)} %get-tuple-element.20.refs_7_) | copy-start | bytes 393220
  70.4 14.4 %copy-start.13 = (s32[1,8,8,2]{2,3,1,0:T(2,128)S(1)}, s32[1,8,8,2]{2,3,1,0:T(2,128)}, u32[]{:S(2)}) copy-start(s32[1,8,8,2]{2,3,1,0:T(2,128)} %param.14) | copy-start | bytes 1540
  93.8 0.9 copy-start.11
  94.7 0.7 copy-start.12
  110.7 1.0 copy-start.4
  111.7 0.7 copy-start.10

commit v4 on v3

--- a/solution.py
+++ b/solution.py
@@ -298,7 +298,7 @@
     leaves = x.shape[1] // width
     steps = next(s for s in (6, 4, 3, 2, 1) if count % s == 0)
     per_step = count // steps
-    unroll = next(s for s in (8, 6, 4, 3, 2, 1) if per_step % s == 0)
+    unroll = next(s for s in (16, 8, 6, 4, 3, 2, 1) if per_step % s == 0)
     shape = (leaves, x.shape[0], width)
 
     def kernel(*refs):

time: 135 us -> 131 us (0.970)
  Pallas kernels: 113 us -> 109 us
    pallas_call x2, Pallas kernels: 28.7 us -> 24.5 us  [local_call(): pl.pallas_call(kernel, grid=(steps,), out_shape=jax.ShapeDtypeStruct(shap...]
where the time goes in v4:
time: 131 us
  Pallas kernels  109 us (83%)
  local copies, waits for them, and re-layouts  18 us (14%)
  other arithmetic  2.72 us (2%)
    pallas_call x2, Pallas kernels, exchange_call(): pl.pallas_call(kernel, out_shape=tuple(shapes), in_specs=specs + [any_spa...  61.7 us
    pallas_call x2, Pallas kernels, local_call(): pl.pallas_call(kernel, grid=(steps,), out_shape=jax.ShapeDtypeStruct(shap...  24.5 us
    pallas_call x2, Pallas kernels, join_call(): pl.pallas_call(kernel, out_shape=(jax.ShapeDtypeStruct((rows, leaves * wi...  16.3 us
    unnamed x36, local copies, waits for them, and re-layouts  12.5 us
    pallas_call x1, Pallas kernels, far_call(): pl.pallas_call(kernel, out_shape=(shape, shape), in_specs=[smem(), smem()...  4.66 us

profile of v4, /device:TPU:0, one launch (start us, length us, event | category | flops | bytes accessed | tf_op | source)
XLA Modules:
  0.0 130.6 jit_solution(4963435313380895250)
XLA Ops:
  0.6 0.8 bitcast_convert_fusion
  1.4 0.1 copy.40
  1.5 0.7 fusion.1
  2.2 0.3 multiply_reduce_fusion
  2.5 2.0 %parent_basis.1 = (bf16[32,2048]{1,0:T(8,128)(2,1)}, bf16[32,32]{1,0:T(8,128)(2,1)}) custom-call(bf16[32,2048]{1,0:T(8,128)(2,1)} %refs_1_.3, bf16[16,32,128]{2,1,0:T(8,128)(2,1)} %refs_2_.1, bf16[16,32,32]{2,1,0:T(8,128)(2,1)} %transfers_ref.1), custom_call_target="tpu_custom_call" | custom-call | flops 10000000 | bytes 1000000 | tf_op jit(solution)/shard_map/parent_basis/pallas_call | solution.py:245
  4.4 0.7 broadcast_in_dim.4
  5.2 0.1 pad.7.clone
  5.3 0.1 maximum_maximum_fusion.refs_5_
  5.4 0.7 copy.42
  6.1 0.8 copy.32
  6.8 0.1 pad_add_fusion
  6.9 0.1 copy.33
  7.0 0.1 copy.34
  7.1 1.6 %copy-done = bf16[1,8,8,128,128]{4,3,2,1,0:T(8,128)(2,1)S(1)} copy-done((bf16[1,8,8,128,128]{4,3,2,1,0:T(8,128)(2,1)S(1)}, bf16[1,8,8,128,128]{4,3,2,1,0:T(8,128)(2,1)}, u32[]{:S(2)}) %copy-start) | copy-done | bytes 2097176
  8.7 0.9 copy-done.2
  9.6 0.9 copy-done.7
  10.5 0.9 copy-done.8
  11.4 46.4 %exchange.2 = (bf16[8,32,2048]{2,1,0:T(8,128)(2,1)S(1)}, bf16[8,16,32,128]{3,2,1,0:T(8,128)(2,1)S(1)}, s32[8,8,128]{2,1,0:T(8,128)S(1)}, bf16[8,8,128,128]{3,2,1...) custom-call(bf16[32,2048]{1,0:T(8,128)(2,1)S(1)} %copy-done.8, ...), custom_call_target="tpu_custom_call" | custom-call | bytes 4000000 | tf_op jit(solution)/shard_map/exchange/pallas_call | solution.py:213
  57.8 0.0 copy-start.1
  57.9 1.3 %copy-done.1 = bf16[8,8,128,128]{3,2,1,0:T(8,128)(2,1)} copy-done((bf16[8,8,128,128]{3,2,1,0:T(8,128)(2,1)}, bf16[8,8,128,128]{3,2,1,0:T(8,128)(2,1)S(1)}, u32[]{:S(2)}) %copy-start.1) | copy-done | bytes 2097176
  59.2 1.0 copy-done.3
  60.2 1.0 copy-done.5
  61.2 0.7 copy-done.9
  61.8 0.1 copy.35
  61.9 0.1 copy.38
  62.0 0.6 reshape.57.refs_1_.refs_3_
  62.6 0.0 copy-done.14
  62.6 0.1 copy.37
  62.7 0.6 reshape.56.refs_0_.refs_2_
  63.4 4.7 %far_blocks.1 = (bf16[8,2,128,128]{3,2,1,0:T(8,128)(2,1)}, bf16[8,2,128,128]{3,2,1,0:T(8,128)(2,1)}) custom-call(s32[32]{0:T(128)} %reshape.56.refs_0_.refs_2_, s32[32]{0:T(128)} %reshape.57.refs_1_.refs_3_, bf16[16,32,128]{2,1,0:T(8,128)(2,1)} %refs_2_.1, bf16[8,2,32,32]{3,2,1,0:T(8,128)(2,1)} %bitcast.24, bf16[8,16,32,128]{3,2,1,0:T(8,128)(2,1)} %copy-done.5, ...), custom_call_target="tpu_custom_call" | custom-call | flops 100000000 | bytes 4000000 | tf_op jit(solution)/shard_map/far_blocks/pallas_call | solution.py:351
  68.0 0.8 add_convert_fusion.refs_6_
  68.8 0.1 copy.36
  68.9 0.7 reshape.55.refs_1_
  69.6 0.0 copy-done.15
  69.6 0.1 copy.39
  69.7 0.7 reshape_squeeze.8.refs_0_
  70.4 12.2 %local_blocks.2.refs_4_ = f32[16,32,128]{2,1,0:T(8,128)} custom-call(s32[576]{0:T(1024)} %reshape_squeeze.8.refs_0_, bf16[32,2048]{1,0:T(8,128)(2,1)} %refs_1_.3, bf16[288,128,128]{2,1,0:T(8,128)(2,1)} %bitcast.29), custom_call_target="tpu_custom_call" | custom-call | flops 9663676416 | bytes 9437184 | tf_op jit(solution)/shard_map/local_blocks/pallas_call | solution.py:307
  82.7 0.0 copy-done.6
  82.7 0.1 copy.30
  82.8 0.7 reshape.53.refs_0_
  83.5 8.1 %near_and_join.2 = (bf16[32,2048]{1,0:T(8,128)(2,1)}, bf16[32,128]{1,0:T(8,128)(2,1)}) custom-call(s32[128]{0:T(128)} %reshape.53.refs_0_, s32[128]{0:T(128)} %reshape.55.refs_1_, s32[32]{0:T(128)} %reshape.56.refs_0_.refs_2_, s32[32]{0:T(128)} %reshape.57.refs_1_.refs_3_, f32[16,32,128]{2,1,0:T(8,128)} %local_blocks.2.refs_4_, ...), custom_call_target="tpu_custom_call" | custom-call | flops 1000000000 | bytes 8000000 | tf_op jit(solution)/shard_map/near_and_join/pallas_call | solution.py:415
  91.7 0.9 copy-done.11
  92.6 0.7 copy-done.12
  93.3 15.3 %exchange.3 = (bf16[8,32,2048]{2,1,0:T(8,128)(2,1)S(1)}, bf16[16,32,128]{2,1,0:T(8,128)(2,1)S(1)}) custom-call(bf16[32,2048]{1,0:T(8,128)(2,1)S(1)} %copy-done.11, bf16[32,128]{1,0:T(8,128)(2,1)S(1)} %copy-done.12), custom_call_target="tpu_custom_call" | custom-call | bytes 4000000 | tf_op jit(solution)/shard_map/exchange/pallas_call | solution.py:213
  108.6 1.0 copy-done.4
  109.5 0.7 copy-done.10
  110.2 12.2 %local_blocks.3.refs_4_ = f32[16,32,128]{2,1,0:T(8,128)} custom-call(s32[576]{0:T(1024)} %reshape_squeeze.8.refs_0_, bf16[32,2048]{1,0:T(8,128)(2,1)} %get-tuple-element.15.refs_1_.refs_0_, bf16[288,128,128]{2,1,0:T(8,128)(2,1)} %bitcast.30), custom_call_target="tpu_custom_call" | custom-call | flops 9663676416 | bytes 9437184 | tf_op jit(solution)/shard_map/local_blocks/pallas_call | solution.py:307
  122.4 8.1 %near_and_join.3 = (bf16[32,2048]{1,0:T(8,128)(2,1)}, bf16[32,128]{1,0:T(8,128)(2,1)}) custom-call(s32[128]{0:T(128)} %reshape.53.refs_0_, s32[128]{0:T(128)} %reshape.55.refs_1_, s32[32]{0:T(128)} %reshape.56.refs_0_.refs_2_, s32[32]{0:T(128)} %reshape.57.refs_1_.refs_3_, f32[16,32,128]{2,1,0:T(8,128)} %local_blocks.3.refs_4_, ...), custom_call_target="tpu_custom_call" | custom-call | flops 1000000000 | bytes 8000000 | tf_op jit(solution)/shard_map/near_and_join/pallas_call | solution.py:415
  (23 shorter events, 0.1 us)
Async XLA Ops:
  2.2 60.4 %copy-start.14 = (s32[1,8,2,2]{1,3,2,0:T(2,128)S(1)}, s32[1,8,2,2]{1,3,2,0:T(2,128)}, u32[]{:S(2)}) copy-start(s32[1,8,2,2]{1,3,2,0:T(2,128)} %param.18) | copy-start | bytes 388
  7.1 1.6 %copy-start = (bf16[1,8,8,128,128]{4,3,2,1,0:T(8,128)(2,1)S(1)}, bf16[1,8,8,128,128]{4,3,2,1,0:T(8,128)(2,1)}, u32[]{:S(2)}) copy-start(bf16[1,8,8,128,128]{4,3,2,1,0:T(8,128)(2,1)} %param.15) | copy-start | bytes 6291460
  8.7 0.9 copy-start.2
  9.6 0.9 copy-start.7
  10.5 0.9 copy-start.8
  11.4 58.2 %copy-start.15 = (s32[1,288,2]{1,2,0:T(2,128)S(1)}, s32[1,288,2]{1,2,0:T(2,128)}, u32[]{:S(2)}) copy-start(s32[1,288,2]{1,2,0:T(2,128)} %param.16) | copy-start | bytes 6916
  57.8 1.3 %copy-start.1 = (bf16[8,8,128,128]{3,2,1,0:T(8,128)(2,1)}, bf16[8,8,128,128]{3,2,1,0:T(8,128)(2,1)S(1)}, u32[]{:S(2)}) copy-start(bf16[8,8,128,128]{3,2,1,0:T(8,128)(2,1)S(1)} %get-tuple-element.26.refs_12_) | copy-start | bytes 6291460
  59.2 1.0 copy-start.3
  60.2 1.0 copy-start.5
  61.2 0.7 copy-start.9
  61.8 20.9 %copy-start.6 = (bf16[16,32,128]{2,1,0:T(8,128)(2,1)}, bf16[16,32,128]{2,1,0:T(8,128)(2,1)S(1)}, u32[]{:S(2)}) copy-start(bf16[16,32,128]{2,1,0:T(8,128)(2,1)S(1)} %get-tuple-element.20.refs_7_) | copy-start | bytes 393220
  70.4 12.2 %copy-start.13 = (s32[1,8,8,2]{2,3,1,0:T(2,128)S(1)}, s32[1,8,8,2]{2,3,1,0:T(2,128)}, u32[]{:S(2)}) copy-start(s32[1,8,8,2]{2,3,1,0:T(2,128)} %param.14) | copy-start | bytes 1540
  91.7 0.9 copy-start.11
  92.6 0.7 copy-start.12
  108.6 1.0 copy-start.4
  109.5 0.7 copy-start.10
